TPU v7x, 512 devices: a whole 4x4x16 slice. The times are simulated.
512 devices in a mesh: dom: 128 (over z, x, core), tile: 4 (over y).
Axes of the slice: x: 4, y: 4, z: 16, core: 2. Of those that a mesh axis runs over, the one named last changes fastest.
Arguments:
- vectors: float32 [4, 16, 131072], P(None, 'tile', 'dom'), may hold values from -6 to 6
- positions: float32 [3, 131072], P(None, 'dom'), may hold values from -8 to 8
- onsite: float32 [4, 131072], P(None, 'dom'), may hold values from -1.5 to 1.5
- neighbors: int32 [4, 131072], P(None, 'dom'), may hold values from 0 to 1280, as said below
Outputs:
- local_gamma: float32 [16, 131072], P('tile', 'dom')
Inputs may be any that keep to these rules, and one draw needn't show every extreme that they name: `neighbors`: bonds are symmetric: if atom i names j then j names i. Codes below 128 appear only on a domain's first 128 slots and codes from 1152 to 1279 only on its last 128 slots (first column only); the number of bonds between two neighbouring domains varies from pair to pair, at most 128, reached by some pair. Slots of a domain that hold no atom have only the code 1024 + 2 * 128; the count of such slots varies between domains.
All inputs are finite; a program needn't handle non-finite values.
Results may differ from a plain program's by a relative error of at most 0.0002.
Values sent between devices are 32-bit elements; how exact they have to be, the bound alone decides.
A program may use at most 64 MiB of HBM per device.

v0:
```python
import jax
import jax.numpy as jnp
from jax import lax
from jax.sharding import PartitionSpec as P

BND = 128
VECS = 16
NMOM = 4


onsite_s = -4.2
onsite_p = 1.72
hop_ss = -2.08
hop_sp = 2.48
hop_pps = 2.72
hop_ppp = -0.72
bond_length = 2.35
energy_scale = 16.0
length_scale = 2.0


def padded_2(array, sides, width):
    for axis, dim in sides:
        devices, length = (lax.axis_size(axis), array.shape[dim])
        up = [(i, (i + 1) % devices) for i in range(devices)]
        down = [(j, i) for i, j in up]
        last = lax.slice_in_dim(array, length - width, length, axis=dim)
        leading = lax.slice_in_dim(array, 0, width, axis=dim)
        before = lax.ppermute(last, axis, up)
        after = lax.ppermute(leading, axis, down)
        array = jnp.concatenate([before, array, after], axis=dim)
    return array


def take_rows(table, index):
    lead = table.shape[:-1]
    flat_rows = table.reshape(-1, table.shape[-1]).T
    picked = jnp.take(flat_rows, index.reshape(-1), axis=0)
    return picked.T.reshape(lead + index.shape)


def slater_koster(offset, bonded):
    distance = jnp.sqrt(jnp.sum(offset * offset, axis=0))
    radial = (
        jnp.exp(-0.5 * (distance - bond_length) * (distance - bond_length)) * bonded / energy_scale
    )
    cosines = offset / jnp.maximum(distance, 1.0)
    block_rows = [
        jnp.stack(
            [
                jnp.full_like(radial, hop_ss),
                hop_sp * cosines[0],
                hop_sp * cosines[1],
                hop_sp * cosines[2],
            ]
        )
    ]
    for row_axis in range(3):
        entries = [-hop_sp * cosines[row_axis]]
        for col_axis in range(3):
            extra = hop_ppp if row_axis == col_axis else 0.0
            entries.append(cosines[row_axis] * cosines[col_axis] * (hop_pps - hop_ppp) + extra)
        block_rows.append(jnp.stack(entries))
    return (jnp.stack(block_rows) * radial, -offset[0] / length_scale)


def build_blocks(padded_pos, own_pos, own_neighbors, none_index):
    partner_pos = take_rows(padded_pos, own_neighbors)
    blocks = []
    drifts = []
    for bond_index in range(4):
        offset = partner_pos[:, bond_index] - own_pos
        bonded = (own_neighbors[bond_index] < none_index).astype(jnp.float32)
        block, drift = slater_koster(offset, bonded)
        blocks.append(block)
        drifts.append(drift)
    return (jnp.stack(blocks), jnp.stack(drifts))


def ghost_rows(field):
    return padded_2(field, (("dom", 2),), BND)


def apply_local(extended, field, blocks, drifts, diagonal, neighbors, kcount):
    padded = jnp.concatenate([extended, jnp.zeros((4, extended.shape[1], 1), jnp.float32)], axis=2)
    beside_all = take_rows(padded, neighbors)
    hsum = jnp.zeros(field.shape, jnp.float32)
    ksum = jnp.zeros((4, kcount, field.shape[2]), jnp.float32)
    for bond_index in range(4):
        beside = beside_all[:, :, bond_index]
        block = blocks[bond_index]
        product = block[:, 0][:, None, :] * beside[0][None]
        for inner in range(1, 4):
            product = product + block[:, inner][:, None, :] * beside[inner][None]
        hsum = hsum + product
        ksum = ksum + drifts[bond_index] * product[:, :kcount]
    return (diagonal[:, None, :] * field + hsum, ksum)


def body(vectors, positions, onsite, neighbors):
    width = vectors.shape[1]
    atoms = positions.shape[1]
    none_index = atoms + 2 * BND
    pos_ghost = padded_2(positions, (("dom", 1),), BND)
    padded_pos = jnp.concatenate([pos_ghost, jnp.zeros((3, 1), jnp.float32)], axis=1)
    blocks, drifts = build_blocks(padded_pos, positions, neighbors, none_index)
    base = jnp.array([onsite_s, onsite_p, onsite_p, onsite_p], jnp.float32)
    diagonal = (base[:, None] + onsite) / energy_scale

    def apply_field(field, kcount):
        return apply_local(ghost_rows(field), field, blocks, drifts, diagonal, neighbors, kcount)

    hv, kv = apply_field(vectors, width)
    a_one, b_zero = (hv, kv)
    hv, kv = apply_field(a_one, width)
    a_two = 2.0 * hv - vectors
    c_one = kv
    hv, kv = apply_field(a_two, width)
    a_three = 2.0 * hv - a_one
    c_two = kv
    hv, kv = apply_field(a_three, width)
    c_three = kv
    hv, kv = apply_field(b_zero, 0)
    b_one = hv
    hv, kv = apply_field(b_one, 0)
    b_two = 2.0 * hv - b_zero
    hv, kv = apply_field(b_two, 0)
    b_three = 2.0 * hv - b_one
    b_stack = jnp.stack([b_zero, b_one, b_two, b_three])
    c_stack = jnp.stack([b_zero, c_one, c_two, c_three])
    terms = jnp.einsum("nopa,mopa->nma", b_stack, c_stack, precision=lax.Precision.HIGHEST)
    terms = -terms.reshape(NMOM * NMOM, atoms) / VECS
    return lax.psum_scatter(terms, "tile", scatter_dimension=0, tiled=True)


def solution(mesh):
    in_specs = (P(None, "tile", "dom"), P(None, "dom"), P(None, "dom"), P(None, "dom"))
    out_specs = P("tile", "dom")
    return jax.shard_map(body, mesh=mesh, in_specs=in_specs, out_specs=out_specs, check_vma=False)
```

profile of v0, /device:TPU:2, one launch (start us, length us, event | category | flops | bytes accessed | tf_op | source)
XLA Modules:
  0.0 345.2 jit_solution(8154813037906361533)
XLA Ops:
  9.2 3.6 %collective-permute-start.1 = (f32[3,128]{1,0:T(4,128)S(1)}, f32[3,128]{1,0:T(4,128)S(1)}, u32[]{:S(2)}, u32[]{:S(2)}) collective-permute-start(f32[3,128]{1,0:T(4,128)S(1)} %get-tuple-element.225), channel_id=1, source_target_pairs={{4,0},{8,4},{12,8},{16,12},{20,16},{24,20},{28,24},{32,28},{36,32}... | collective-permute-start | bytes 4616 | tf_op jit(solution)/shard_map/ppermute | solution.py:30
  15.4 6.2 %collective-permute-start.3 = (f32[4,4,128]{2,1,0:T(4,128)S(1)}, f32[4,4,128]{2,1,0:T(4,128)S(1)}, u32[]{:S(2)}, u32[]{:S(2)}) collective-permute-start(f32[4,4,128]{2,1,0:T(4,128)S(1)} %get-tuple-element.169), channel_id=1, source_target_pairs={{4,0},{8,4},{12,8},{16,12},{20,16},{24,20},{28,24},{32,28},{36,32}... | collective-permute-start | bytes 24584 | tf_op jit(solution)/shard_map/ppermute | solution.py:30
  26.6 10.8 %gather_fusion = f32[4096,3]{1,0:T(8,128)S(1)} fusion(f32[1281,3]{1,0:T(8,128)S(1)} %bitcast.468, s32[4096]{0:T(1024)S(1)} %broadcast_clamp_fusion), kind=kCustom, calls=%fused_computation.7 | custom fusion | bytes 114688 | tf_op jit(solution)/shard_map/jit(_take)/gather | solution.py:38
  42.2 14.1 %gather_fusion.1 = f32[4096,16]{1,0:T(8,128)} fusion(f32[1281,16]{1,0:T(8,128)S(1)} %bitcast.470, s32[4096]{0:T(1024)S(1)} %fusion.6), kind=kCustom, calls=%fused_computation.clone | custom fusion | bytes 540672 | tf_op jit(solution)/shard_map/jit(_take)/gather | solution.py:38
  56.3 3.6 %select_bitcast_fusion.6 = f32[16,4096]{0,1:T(8,128)S(1)} fusion(f32[4096,16]{1,0:T(8,128)} %gather_fusion.1, pred[4096]{0:T(1024)(128)(4,1)S(1)} %compare_and_fusion), kind=kLoop, calls=%fused_computation.17 | loop fusion | flops 65536 | bytes 528384 | tf_op jit(solution)/shard_map/transpose | solution.py:39
  63.1 7.7 %collective-permute-start.5 = (f32[4,4,128]{2,1,0:T(4,128)S(1)}, f32[4,4,128]{2,1,0:T(4,128)S(1)}, u32[]{:S(2)}, u32[]{:S(2)}) collective-permute-start(f32[4,4,128]{2,1,0:T(4,128)S(1)} %get-tuple-element.145), channel_id=1, source_target_pairs={{4,0},{8,4},{12,8},{16,12},{20,16},{24,20},{28,24},{32,28},{36,32}... | collective-permute-start | bytes 24584 | tf_op jit(solution)/shard_map/ppermute | solution.py:30
  73.0 7.0 %collective-permute-start.11 = (f32[4,4,128]{2,1,0:T(4,128)S(1)}, f32[4,4,128]{2,1,0:T(4,128)S(1)}, u32[]{:S(2)}, u32[]{:S(2)}) collective-permute-start(f32[4,4,128]{2,1,0:T(4,128)S(1)} %get-tuple-element.151), channel_id=1, source_target_pairs={{4,0},{8,4},{12,8},{16,12},{20,16},{24,20},{28,24},{32,28},{36,32}... | collective-permute-start | bytes 24584 | tf_op jit(solution)/shard_map/ppermute | solution.py:30
  80.3 14.1 %gather_fusion.2 = f32[4096,16]{1,0:T(8,128)} fusion(f32[1281,16]{1,0:T(8,128)S(1)} %bitcast.471, s32[4096]{0:T(1024)S(1)} %fusion.6), kind=kCustom, calls=%fused_computation.1.clone | custom fusion | bytes 540672 | tf_op jit(solution)/shard_map/jit(_take)/gather | solution.py:38
  94.4 3.6 %select_bitcast_fusion.5 = f32[16,4096]{0,1:T(8,128)S(1)} fusion(f32[4096,16]{1,0:T(8,128)} %gather_fusion.2, pred[4096]{0:T(1024)(128)(4,1)S(1)} %compare_and_fusion), kind=kLoop, calls=%fused_computation.16 | loop fusion | flops 65536 | bytes 528384 | tf_op jit(solution)/shard_map/transpose | solution.py:39
  101.6 7.0 %collective-permute-start.7 = (f32[4,4,128]{2,1,0:T(4,128)S(1)}, f32[4,4,128]{2,1,0:T(4,128)S(1)}, u32[]{:S(2)}, u32[]{:S(2)}) collective-permute-start(f32[4,4,128]{2,1,0:T(4,128)S(1)} %get-tuple-element.143), channel_id=1, source_target_pairs={{4,0},{8,4},{12,8},{16,12},{20,16},{24,20},{28,24},{32,28},{36,32}... | collective-permute-start | bytes 24584 | tf_op jit(solution)/shard_map/ppermute | solution.py:30
  110.2 14.1 %gather_fusion.3 = f32[4096,16]{1,0:T(8,128)} fusion(f32[1281,16]{1,0:T(8,128)S(1)} %bitcast.472, s32[4096]{0:T(1024)S(1)} %fusion.6), kind=kCustom, calls=%fused_computation.2.clone | custom fusion | bytes 540672 | tf_op jit(solution)/shard_map/jit(_take)/gather | solution.py:38
  124.3 3.6 %select_bitcast_fusion.4 = f32[16,4096]{0,1:T(8,128)S(1)} fusion(f32[4096,16]{1,0:T(8,128)} %gather_fusion.3, pred[4096]{0:T(1024)(128)(4,1)S(1)} %compare_and_fusion), kind=kLoop, calls=%fused_computation.15 | loop fusion | flops 65536 | bytes 528384 | tf_op jit(solution)/shard_map/transpose | solution.py:39
  131.5 6.7 %collective-permute-start.9 = (f32[4,4,128]{2,1,0:T(4,128)S(1)}, f32[4,4,128]{2,1,0:T(4,128)S(1)}, u32[]{:S(2)}, u32[]{:S(2)}) collective-permute-start(f32[4,4,128]{2,1,0:T(4,128)S(1)} %get-tuple-element.141), channel_id=1, source_target_pairs={{4,0},{8,4},{12,8},{16,12},{20,16},{24,20},{28,24},{32,28},{36,32}... | collective-permute-start | bytes 24584 | tf_op jit(solution)/shard_map/ppermute | solution.py:30
  139.6 14.1 %gather_fusion.5 = f32[4096,16]{1,0:T(8,128)} fusion(f32[1281,16]{1,0:T(8,128)S(1)} %bitcast.473, s32[4096]{0:T(1024)S(1)} %fusion.6), kind=kCustom, calls=%fused_computation.4.clone | custom fusion | bytes 540672 | tf_op jit(solution)/shard_map/jit(_take)/gather | solution.py:38
  154.0 14.1 %gather_fusion.4 = f32[4096,16]{1,0:T(8,128)} fusion(f32[1281,16]{1,0:T(8,128)S(1)} %bitcast.474, s32[4096]{0:T(1024)S(1)} %fusion.6), kind=kCustom, calls=%fused_computation.3.clone | custom fusion | bytes 540672 | tf_op jit(solution)/shard_map/jit(_take)/gather | solution.py:38
  177.5 7.2 %collective-permute-start.13 = (f32[4,4,128]{2,1,0:T(4,128)S(1)}, f32[4,4,128]{2,1,0:T(4,128)S(1)}, u32[]{:S(2)}, u32[]{:S(2)}) collective-permute-start(f32[4,4,128]{2,1,0:T(4,128)S(1)} %get-tuple-element.149), channel_id=1, source_target_pairs={{4,0},{8,4},{12,8},{16,12},{20,16},{24,20},{28,24},{32,28},{36,32}... | collective-permute-start | bytes 24584 | tf_op jit(solution)/shard_map/ppermute | solution.py:30
  187.8 14.1 %gather_fusion.6 = f32[4096,16]{1,0:T(8,128)} fusion(f32[1281,16]{1,0:T(8,128)S(1)} %bitcast.475, s32[4096]{0:T(1024)S(1)} %fusion.6), kind=kCustom, calls=%fused_computation.5.clone | custom fusion | bytes 540672 | tf_op jit(solution)/shard_map/jit(_take)/gather | solution.py:38
  209.4 7.5 %collective-permute-start.15 = (f32[4,4,128]{2,1,0:T(4,128)S(1)}, f32[4,4,128]{2,1,0:T(4,128)S(1)}, u32[]{:S(2)}, u32[]{:S(2)}) collective-permute-start(f32[4,4,128]{2,1,0:T(4,128)S(1)} %get-tuple-element.147), channel_id=1, source_target_pairs={{4,0},{8,4},{12,8},{16,12},{20,16},{24,20},{28,24},{32,28},{36,32}... | collective-permute-start | bytes 24584 | tf_op jit(solution)/shard_map/ppermute | solution.py:30
  218.3 14.1 %gather_fusion.7 = f32[4096,16]{1,0:T(8,128)} fusion(f32[1281,16]{1,0:T(8,128)S(1)} %bitcast.469, s32[4096]{0:T(1024)S(1)} %fusion.6), kind=kCustom, calls=%fused_computation.6.clone | custom fusion | bytes 540672 | tf_op jit(solution)/shard_map/jit(_take)/gather | solution.py:38
  232.4 3.6 %select_bitcast_fusion = f32[16,4096]{0,1:T(8,128)S(1)} fusion(f32[4096,16]{1,0:T(8,128)} %gather_fusion.7, pred[4096]{0:T(1024)(128)(4,1)S(1)} %compare_and_fusion), kind=kLoop, calls=%fused_computation.11 | loop fusion | flops 65536 | bytes 528384 | tf_op jit(solution)/shard_map/transpose | solution.py:39
  239.4 6.3 %copy.399 = f32[4,4,4,1024]{2,0,1,3:T(4,128)} copy(f32[4,4,4,1024]{3,2,1,0:T(4,128)S(1)} %get-tuple-element.139) | data formatting | bytes 524288 | tf_op jit(solution)/shard_map/stack | solution.py:130
  245.7 6.2 %copy.400 = f32[4,4,4,1024]{2,0,1,3:T(4,128)} copy(f32[4,4,4,1024]{3,2,1,0:T(4,128)S(1)} %get-tuple-element.138) | data formatting | bytes 524288 | tf_op jit(solution)/shard_map/stack | solution.py:129
  251.9 19.4 %fusion.1 = f32[4,4,1024]{0,1,2:T(4,128)S(1)} fusion(f32[4,4,4,1024]{2,0,1,3:T(4,128)} %copy.399, f32[4,4,4,1024]{2,0,1,3:T(4,128)} %copy.400), kind=kOutput, calls=%fused_computation.10 | convolution fusion | flops 3178496 | bytes 589824 | tf_op jit(solution)/shard_map/nopa,mopa->nma/dot_general | solution.py:131
  274.8 62.3 %all-reduce.3.cloned.1.call-done = f32[16,1024]{1,0:T(8,128)} async-done(((f32[16,1024]{1,0:T(8,128)}), f32[16,1024]{1,0:T(8,128)}) %all-reduce.3.cloned.1.call-update) | async-done | bytes 65552
  (303 shorter events, 58.5 us)
Async XLA Ops:
  6.5 330.5 %all-reduce.3.cloned.1.call-start = ((), (), s32[]{:S(2)}) async-start(), calls=%async_computation | async-start | bytes 131072
  7.2 18.4 %collective-permute-start = (f32[3,128]{1,0:T(4,128)S(1)}, f32[3,128]{1,0:T(4,128)S(1)}, u32[]{:S(2)}, u32[]{:S(2)}) collective-permute-start(f32[3,128]{1,0:T(4,128)S(1)} %get-tuple-element.224), channel_id=1, source_target_pairs={{0,4},{4,8},{8,12},{12,16},{16,20},{20,24},{24,28},{28,32},{32,36}... | collective-permute-start | bytes 4616 | tf_op jit(solution)/shard_map/ppermute | solution.py:29
  9.2 16.5 %collective-permute-start.1 = (f32[3,128]{1,0:T(4,128)S(1)}, f32[3,128]{1,0:T(4,128)S(1)}, u32[]{:S(2)}, u32[]{:S(2)}) collective-permute-start(f32[3,128]{1,0:T(4,128)S(1)} %get-tuple-element.225), channel_id=1, source_target_pairs={{4,0},{8,4},{12,8},{16,12},{20,16},{24,20},{28,24},{32,28},{36,32}... | collective-permute-start | bytes 4616 | tf_op jit(solution)/shard_map/ppermute | solution.py:30
  13.5 28.3 %collective-permute-start.2 = (f32[4,4,128]{2,1,0:T(4,128)S(1)}, f32[4,4,128]{2,1,0:T(4,128)S(1)}, u32[]{:S(2)}, u32[]{:S(2)}) collective-permute-start(f32[4,4,128]{2,1,0:T(4,128)S(1)} %get-tuple-element.168), channel_id=1, source_target_pairs={{0,4},{4,8},{8,12},{12,16},{16,20},{20,24},{24,28},{28,32},{32,36}... | collective-permute-start | bytes 24584 | tf_op jit(solution)/shard_map/ppermute | solution.py:29
  15.4 26.4 %collective-permute-start.3 = (f32[4,4,128]{2,1,0:T(4,128)S(1)}, f32[4,4,128]{2,1,0:T(4,128)S(1)}, u32[]{:S(2)}, u32[]{:S(2)}) collective-permute-start(f32[4,4,128]{2,1,0:T(4,128)S(1)} %get-tuple-element.169), channel_id=1, source_target_pairs={{4,0},{8,4},{12,8},{16,12},{20,16},{24,20},{28,24},{32,28},{36,32}... | collective-permute-start | bytes 24584 | tf_op jit(solution)/shard_map/ppermute | solution.py:30
  61.2 18.7 %collective-permute-start.4 = (f32[4,4,128]{2,1,0:T(4,128)S(1)}, f32[4,4,128]{2,1,0:T(4,128)S(1)}, u32[]{:S(2)}, u32[]{:S(2)}) collective-permute-start(f32[4,4,128]{2,1,0:T(4,128)S(1)} %get-tuple-element.144), channel_id=1, source_target_pairs={{0,4},{4,8},{8,12},{12,16},{16,20},{20,24},{24,28},{28,32},{32,36}... | collective-permute-start | bytes 24584 | tf_op jit(solution)/shard_map/ppermute | solution.py:29
  63.1 16.8 %collective-permute-start.5 = (f32[4,4,128]{2,1,0:T(4,128)S(1)}, f32[4,4,128]{2,1,0:T(4,128)S(1)}, u32[]{:S(2)}, u32[]{:S(2)}) collective-permute-start(f32[4,4,128]{2,1,0:T(4,128)S(1)} %get-tuple-element.145), channel_id=1, source_target_pairs={{4,0},{8,4},{12,8},{16,12},{20,16},{24,20},{28,24},{32,28},{36,32}... | collective-permute-start | bytes 24584 | tf_op jit(solution)/shard_map/ppermute | solution.py:30
  71.1 67.9 %collective-permute-start.10 = (f32[4,4,128]{2,1,0:T(4,128)S(1)}, f32[4,4,128]{2,1,0:T(4,128)S(1)}, u32[]{:S(2)}, u32[]{:S(2)}) collective-permute-start(f32[4,4,128]{2,1,0:T(4,128)S(1)} %get-tuple-element.150), channel_id=1, source_target_pairs={{0,4},{4,8},{8,12},{12,16},{16,20},{20,24},{24,28},{28,32},{32,36}... | collective-permute-start | bytes 24584 | tf_op jit(solution)/shard_map/ppermute | solution.py:29
  73.0 66.0 %collective-permute-start.11 = (f32[4,4,128]{2,1,0:T(4,128)S(1)}, f32[4,4,128]{2,1,0:T(4,128)S(1)}, u32[]{:S(2)}, u32[]{:S(2)}) collective-permute-start(f32[4,4,128]{2,1,0:T(4,128)S(1)} %get-tuple-element.151), channel_id=1, source_target_pairs={{4,0},{8,4},{12,8},{16,12},{20,16},{24,20},{28,24},{32,28},{36,32}... | collective-permute-start | bytes 24584 | tf_op jit(solution)/shard_map/ppermute | solution.py:30
  99.6 9.8 %collective-permute-start.6 = (f32[4,4,128]{2,1,0:T(4,128)S(1)}, f32[4,4,128]{2,1,0:T(4,128)S(1)}, u32[]{:S(2)}, u32[]{:S(2)}) collective-permute-start(f32[4,4,128]{2,1,0:T(4,128)S(1)} %get-tuple-element.142), channel_id=1, source_target_pairs={{0,4},{4,8},{8,12},{12,16},{16,20},{20,24},{24,28},{28,32},{32,36}... | collective-permute-start | bytes 24584 | tf_op jit(solution)/shard_map/ppermute | solution.py:29
  101.6 8.3 %collective-permute-start.7 = (f32[4,4,128]{2,1,0:T(4,128)S(1)}, f32[4,4,128]{2,1,0:T(4,128)S(1)}, u32[]{:S(2)}, u32[]{:S(2)}) collective-permute-start(f32[4,4,128]{2,1,0:T(4,128)S(1)} %get-tuple-element.143), channel_id=1, source_target_pairs={{4,0},{8,4},{12,8},{16,12},{20,16},{24,20},{28,24},{32,28},{36,32}... | collective-permute-start | bytes 24584 | tf_op jit(solution)/shard_map/ppermute | solution.py:30
  129.5 9.5 %collective-permute-start.8 = (f32[4,4,128]{2,1,0:T(4,128)S(1)}, f32[4,4,128]{2,1,0:T(4,128)S(1)}, u32[]{:S(2)}, u32[]{:S(2)}) collective-permute-start(f32[4,4,128]{2,1,0:T(4,128)S(1)} %get-tuple-element.140), channel_id=1, source_target_pairs={{0,4},{4,8},{8,12},{12,16},{16,20},{20,24},{24,28},{28,32},{32,36}... | collective-permute-start | bytes 24584 | tf_op jit(solution)/shard_map/ppermute | solution.py:29
  131.5 7.8 %collective-permute-start.9 = (f32[4,4,128]{2,1,0:T(4,128)S(1)}, f32[4,4,128]{2,1,0:T(4,128)S(1)}, u32[]{:S(2)}, u32[]{:S(2)}) collective-permute-start(f32[4,4,128]{2,1,0:T(4,128)S(1)} %get-tuple-element.141), channel_id=1, source_target_pairs={{4,0},{8,4},{12,8},{16,12},{20,16},{24,20},{28,24},{32,28},{36,32}... | collective-permute-start | bytes 24584 | tf_op jit(solution)/shard_map/ppermute | solution.py:30
  175.5 11.9 %collective-permute-start.12 = (f32[4,4,128]{2,1,0:T(4,128)S(1)}, f32[4,4,128]{2,1,0:T(4,128)S(1)}, u32[]{:S(2)}, u32[]{:S(2)}) collective-permute-start(f32[4,4,128]{2,1,0:T(4,128)S(1)} %get-tuple-element.148), channel_id=1, source_target_pairs={{0,4},{4,8},{8,12},{12,16},{16,20},{20,24},{24,28},{28,32},{32,36}... | collective-permute-start | bytes 24584 | tf_op jit(solution)/shard_map/ppermute | solution.py:29
  177.5 10.0 %collective-permute-start.13 = (f32[4,4,128]{2,1,0:T(4,128)S(1)}, f32[4,4,128]{2,1,0:T(4,128)S(1)}, u32[]{:S(2)}, u32[]{:S(2)}) collective-permute-start(f32[4,4,128]{2,1,0:T(4,128)S(1)} %get-tuple-element.149), channel_id=1, source_target_pairs={{4,0},{8,4},{12,8},{16,12},{20,16},{24,20},{28,24},{32,28},{36,32}... | collective-permute-start | bytes 24584 | tf_op jit(solution)/shard_map/ppermute | solution.py:30
  206.6 11.4 %copy-start.10 = (f32[1,4,1,1024]{3,1,2,0:T(4,128)}, f32[1,4,1,1024]{3,1,2,0:T(4,128)S(1)}, u32[]{:S(2)}) copy-start(f32[1,4,1,1024]{3,1,2,0:T(4,128)S(1)} %copy.693) | copy-start | bytes 49156
  206.6 11.4 %copy-start.11 = (f32[1,4,1,1024]{3,1,2,0:T(4,128)}, f32[1,4,1,1024]{3,1,2,0:T(4,128)S(1)}, u32[]{:S(2)}) copy-start(f32[1,4,1,1024]{3,1,2,0:T(4,128)S(1)} %copy.694) | copy-start | bytes 49156
  206.7 11.4 %copy-start.12 = (f32[1,4,1,1024]{3,1,2,0:T(4,128)}, f32[1,4,1,1024]{3,1,2,0:T(4,128)S(1)}, u32[]{:S(2)}) copy-start(f32[1,4,1,1024]{3,1,2,0:T(4,128)S(1)} %copy.695) | copy-start | bytes 49156
  206.7 25.7 %copy-start.15 = (f32[1,4,1,1024]{3,1,2,0:T(4,128)}, f32[1,4,1,1024]{3,1,2,0:T(4,128)S(1)}, u32[]{:S(2)}) copy-start(f32[1,4,1,1024]{3,1,2,0:T(4,128)S(1)} %copy.698) | copy-start | bytes 49156
  206.8 25.7 %copy-start.16 = (f32[1,4,1,1024]{3,1,2,0:T(4,128)}, f32[1,4,1,1024]{3,1,2,0:T(4,128)S(1)}, u32[]{:S(2)}) copy-start(f32[1,4,1,1024]{3,1,2,0:T(4,128)S(1)} %copy.699) | copy-start | bytes 49156
  206.8 25.7 %copy-start.17 = (f32[1,4,1,1024]{3,1,2,0:T(4,128)}, f32[1,4,1,1024]{3,1,2,0:T(4,128)S(1)}, u32[]{:S(2)}) copy-start(f32[1,4,1,1024]{3,1,2,0:T(4,128)S(1)} %copy.700) | copy-start | bytes 49156
  206.8 25.6 %copy-start.18 = (f32[1,4,1,1024]{3,1,2,0:T(4,128)}, f32[1,4,1,1024]{3,1,2,0:T(4,128)S(1)}, u32[]{:S(2)}) copy-start(f32[1,4,1,1024]{3,1,2,0:T(4,128)S(1)} %copy.701) | copy-start | bytes 49156
  207.5 9.7 %collective-permute-start.14 = (f32[4,4,128]{2,1,0:T(4,128)S(1)}, f32[4,4,128]{2,1,0:T(4,128)S(1)}, u32[]{:S(2)}, u32[]{:S(2)}) collective-permute-start(f32[4,4,128]{2,1,0:T(4,128)S(1)} %get-tuple-element.146), channel_id=1, source_target_pairs={{0,4},{4,8},{8,12},{12,16},{16,20},{20,24},{24,28},{28,32},{32,36}... | collective-permute-start | bytes 24584 | tf_op jit(solution)/shard_map/ppermute | solution.py:29
  209.4 8.6 %collective-permute-start.15 = (f32[4,4,128]{2,1,0:T(4,128)S(1)}, f32[4,4,128]{2,1,0:T(4,128)S(1)}, u32[]{:S(2)}, u32[]{:S(2)}) collective-permute-start(f32[4,4,128]{2,1,0:T(4,128)S(1)} %get-tuple-element.147), channel_id=1, source_target_pairs={{4,0},{8,4},{12,8},{16,12},{20,16},{24,20},{28,24},{32,28},{36,32}... | collective-permute-start | bytes 24584 | tf_op jit(solution)/shard_map/ppermute | solution.py:30
  (17 other events, 139.1 us)
Sparse Core Ops, SparseCore 0:
  273.0 64.0 all-reduce.2
where the time goes:
time: 347 us; the launch traced here: 345 us
  local copies, waits for them, and re-layouts  143 us (41%)
  starting transfers between devices  68.1 us (20%)
  waiting for transfers between devices  63.9 us (18%)
  other arithmetic  35 us (10%)
  matrix products  19.4 us (6%)
  between operations  16.1 us (5%)
    gather x8, local copies, waits for them, and re-layouts, take_rows(): picked = jnp.take(flat_rows, index.reshape(-1), axis=0)  109 us
    unnamed x2, waiting for transfers between devices  62.3 us
    ppermute x8, starting transfers between devices, padded_2(): after = lax.ppermute(leading, axis, down)  52.7 us
    transpose x6, other arithmetic, take_rows(): return picked.T.reshape(lead + index.shape)  21.5 us
    dot_general x1, matrix products, body(): jnp.einsum('nopa,mopa->nma', b_stack, c_stack, precision=lax.Precision.HI...  19.4 us
    ppermute x8, starting transfers between devices, padded_2(): before = lax.ppermute(last, axis, up)  15.3 us
    unnamed x175, local copies, waits for them, and re-layouts  7.39 us
  transfers between devices with their start and end apart: 17, of which 4 were waited for; matrix products, arithmetic and copies ran while one was open for 19% of the time, Pallas kernels for 0%

commit v1 on v0

v1 whole, which is shorter than its diff:
```python
import jax
import jax.numpy as jnp
from jax import lax
from jax.experimental import pallas as pl
from jax.experimental.pallas import tpu as pltpu
from jax.sharding import PartitionSpec as P

BND = 128
VECS = 16
NMOM = 4
NORB = 4
LANES = 128
GROUPS = 8

onsite_s = -4.2
onsite_p = 1.72
hop_ss = -2.08
hop_sp = 2.48
hop_pps = 2.72
hop_ppp = -0.72
bond_length = 2.35
energy_scale = 16.0
length_scale = 2.0

MESH = pl.DeviceIdType.MESH
F32 = jnp.float32
TILE = (GROUPS, LANES)


def lanes_of(source, index):
    return jnp.take_along_axis(source, index, axis=1, mode="promise_in_bounds")


def pick(bits, options):
    for bit in bits:
        options = [jnp.where(bit, options[i + 1], options[i]) for i in range(0, len(options), 2)]
    return options[0]


def kernel(
    ndom, ntile,
    vec_hbm, pos_hbm, ons_hbm, nei_hbm, out_ref,
    vec_in, pos_in, ons_in, nei_in,
    pos, diag, code, low, geo, a_all, b_all, c_all, h_a, h_b, k_a,
    send0, send, ghost0, ghost, mom, mom_in,
    in_sem, halo_send, halo_recv, mom_send, mom_recv,
):
    dom, tile = lax.axis_index("dom"), lax.axis_index("tile")
    up, down = lax.rem(dom + 1, ndom), lax.rem(dom + ndom - 1, ndom)

    barrier = pltpu.get_barrier_semaphore()
    for other in (up, down):
        pl.semaphore_signal(barrier, inc=1, device_id={"dom": other}, device_id_type=MESH)
    for step in range(1, ntile):
        peer = lax.rem(tile + step, ntile)
        pl.semaphore_signal(barrier, inc=1, device_id={"tile": peer}, device_id_type=MESH)

    loads = [
        pltpu.make_async_copy(source, target, in_sem.at[i])
        for i, (source, target) in enumerate(
            ((vec_hbm, vec_in), (pos_hbm, pos_in), (nei_hbm, nei_in), (ons_hbm, ons_in))
        )
    ]
    for load in loads:
        load.start()
    for load in loads:
        load.wait()

    for group in range(GROUPS):
        cut = pl.ds(group * LANES, LANES)
        for orbital in range(NORB):
            a_all[0, pl.ds(orbital * 4, 4), group, :] = vec_in[orbital, :, cut]
        pos[:, group, :] = pos_in[:, cut]
        diag[:, group, :] = ons_in[:, cut]
        code[:, group, :] = nei_in[:, cut]
    for side, group in ((0, 0), (1, GROUPS - 1)):
        cut = pl.ds(group * LANES, LANES)
        for orbital in range(NORB):
            send0[side, pl.ds(orbital * 4, 4), :] = vec_in[orbital, :, cut]
        send0[side, pl.ds(16, 3), :] = pos_in[:, cut]

    def halo(step):
        copies = []
        for side, other in ((0, down), (1, up)):
            source, target = (send0.at[side], ghost0.at[1 - side]) if step == 0 else (
                send.at[step - 1, side], ghost.at[step - 1, 1 - side])
            copies.append(pltpu.make_async_remote_copy(
                src_ref=source, dst_ref=target,
                send_sem=halo_send.at[step, side], recv_sem=halo_recv.at[step, 1 - side],
                device_id={"dom": other}, device_id_type=MESH,
            ))
        return copies

    pl.semaphore_wait(barrier, 2 + ntile - 1)
    halos = [halo(step) for step in range(NMOM)]
    for copy in halos[0]:
        copy.start()

    for orbital in range(NORB):
        base = onsite_s if orbital == 0 else onsite_p
        diag[orbital] = (base + diag[orbital]) / energy_scale
    for bond in range(4):
        low[bond] = jnp.bitwise_and(code[bond], LANES - 1)
        code[bond] = lax.shift_right_logical(code[bond], 7) - 1

    def masks():
        return [[jnp.bitwise_and(code[bond], 1 << bit) != 0 for bit in range(3)] for bond in range(4)]

    def gather(ref, *row):
        bits = masks()
        found = [[] for _ in range(4)]
        for group in range(GROUPS):
            source = jnp.broadcast_to(ref[(*row, pl.ds(group, 1), slice(None))], TILE)
            for bond in range(4):
                found[bond].append(lanes_of(source, low[bond]))
        return [pick(bits[bond], found[bond]) for bond in range(4)]

    def gather_ghost(ref, *row):
        below = jnp.broadcast_to(ref[(0, pl.ds(*row, 1), slice(None))], TILE)
        above = jnp.broadcast_to(ref[(1, pl.ds(*row, 1), slice(None))], TILE)
        upper_half = lax.broadcasted_iota(jnp.int32, TILE, 0) >= GROUPS // 2
        return lanes_of(jnp.where(upper_half, above, below), low[0])

    def put_geometry(slot, partner, bonded):
        offset = [partner[axis] - pos[axis] for axis in range(3)]
        distance = jnp.sqrt(offset[0] * offset[0] + offset[1] * offset[1] + offset[2] * offset[2])
        away = distance - bond_length
        radial = jnp.where(bonded, jnp.exp(-0.5 * away * away) / energy_scale, 0.0)
        inverse = 1.0 / jnp.maximum(distance, 1.0)
        geo[slot, 0] = hop_ss * radial
        geo[slot, 1] = hop_sp * radial
        geo[slot, 2] = (hop_pps - hop_ppp) * radial
        geo[slot, 3] = hop_ppp * radial
        for axis in range(3):
            geo[slot, 4 + axis] = offset[axis] * inverse
        geo[slot, 7] = offset[0] * (-1.0 / length_scale)

    def hop(slot, beside):
        along = geo[slot, 4] * beside[1] + geo[slot, 5] * beside[2] + geo[slot, 6] * beside[3]
        mixed = geo[slot, 2] * along - geo[slot, 1] * beside[0]
        result = [geo[slot, 0] * beside[0] + geo[slot, 1] * along]
        for axis in range(3):
            result.append(geo[slot, 4 + axis] * mixed + geo[slot, 3] * beside[1 + axis])
        return result

    partner = [gather(pos, axis) for axis in range(3)]
    for bond in range(4):
        inside = jnp.logical_and(code[bond] >= 0, code[bond] < GROUPS)
        put_geometry(bond, [partner[axis][bond] for axis in range(3)], inside)

    for step in range(NMOM):
        has_b, last = step > 0, step == NMOM - 1

        def inner(vector, carry):
            beside = [gather(a_all, step, orbital * 4 + vector) for orbital in range(NORB)]
            hsum, ksum = [None] * NORB, [None] * NORB
            for bond in range(4):
                term = hop(bond, [beside[orbital][bond] for orbital in range(NORB)])
                drift = geo[bond, 7]
                for orbital in range(NORB):
                    moved = drift * term[orbital]
                    hsum[orbital] = term[orbital] if bond == 0 else hsum[orbital] + term[orbital]
                    ksum[orbital] = moved if bond == 0 else ksum[orbital] + moved
            for orbital in range(NORB):
                if not last:
                    h_a[orbital * 4 + vector] = hsum[orbital]
                k_a[orbital * 4 + vector] = ksum[orbital]
            if has_b:
                beside = [gather(b_all, step - 1, orbital * 4 + vector) for orbital in range(NORB)]
                for bond in range(4):
                    term = hop(bond, [beside[orbital][bond] for orbital in range(NORB)])
                    for orbital in range(NORB):
                        hsum[orbital] = term[orbital] if bond == 0 else hsum[orbital] + term[orbital]
                for orbital in range(NORB):
                    h_b[orbital * 4 + vector] = hsum[orbital]
            return carry

        lax.fori_loop(0, 4, inner, 0)

        for copy in halos[step]:
            copy.wait_recv()
        incoming = ghost0 if step == 0 else ghost.at[step - 1]
        if step == 0:
            outside = jnp.logical_or(code[0] == -1, code[0] == GROUPS)
            put_geometry(4, [gather_ghost(ghost0, 16 + axis) for axis in range(3)], outside)

        def outer(vector, carry):
            rows = [orbital * 4 + vector for orbital in range(NORB)]
            term = hop(4, [gather_ghost(incoming, row) for row in rows])
            drift = geo[4, 7]
            for orbital, row in enumerate(rows):
                moved = k_a[row] + drift * term[orbital]
                if step == 0:
                    b_all[0, row] = moved
                c_all[step, row] = moved
                if not last:
                    value = diag[orbital] * a_all[step, row] + (h_a[row] + term[orbital])
                    if step > 0:
                        value = 2.0 * value - a_all[step - 1, row]
                    a_all[step + 1, row] = value
                    ends = [(value, row)] + ([(moved, 16 + row)] if step == 0 else [])
                    for end, place in ends:
                        send[step, 0, pl.ds(place, 1), :] = end[0:1]
                        send[step, 1, pl.ds(place, 1), :] = end[GROUPS - 1:]
            if has_b:
                term = hop(4, [gather_ghost(incoming, 16 + row) for row in rows])
                for orbital, row in enumerate(rows):
                    value = diag[orbital] * b_all[step - 1, row] + (h_b[row] + term[orbital])
                    if step > 1:
                        value = 2.0 * value - b_all[step - 2, row]
                    b_all[step, row] = value
                    if not last:
                        send[step, 0, pl.ds(16 + row, 1), :] = value[0:1]
                        send[step, 1, pl.ds(16 + row, 1), :] = value[GROUPS - 1:]
            return carry

        lax.fori_loop(0, 4, outer, 0)
        if not last:
            for copy in halos[step + 1]:
                copy.start()

        pairs = [(step, m) for m in range(step + 1)] + [(n, step) for n in range(step)]

        def moments(row, sums):
            b_rows = [b_all[n, row] for n in range(step + 1)]
            c_rows = [c_all[m, row] for m in range(step + 1)]
            return tuple(total + b_rows[n] * c_rows[m] for total, (n, m) in zip(sums, pairs))

        sums = lax.fori_loop(0, 16, moments, tuple(jnp.zeros(TILE, F32) for _ in pairs))
        for (n, m), total in zip(pairs, sums):
            mom[n, m] = total

    copies = []
    for step in range(1, ntile):
        peer = lax.rem(tile + step, ntile)
        copies.append(pltpu.make_async_remote_copy(
            src_ref=mom.at[peer], dst_ref=mom_in.at[step - 1],
            send_sem=mom_send.at[step - 1], recv_sem=mom_recv.at[step - 1],
            device_id={"tile": peer}, device_id_type=MESH,
        ))
    for copy in copies:
        copy.start()
    for copy in copies:
        copy.wait_recv()
    for m in range(NMOM):
        total = mom[tile, m]
        for other in range(ntile - 1):
            total = total + mom_in[other, m]
        out_ref[m] = total * (-1.0 / VECS)
    for group in halos + [copies]:
        for copy in group:
            copy.wait_send()


def body(ndom, ntile, vectors, positions, onsite, neighbors):
    import functools
    rows = NORB * vectors.shape[1]
    hbm = pl.BlockSpec(memory_space=pltpu.HBM)
    tiles = lambda *lead: pltpu.VMEM((*lead, *TILE), F32)
    result = pl.pallas_call(
        functools.partial(kernel, ndom, ntile),
        out_shape=jax.ShapeDtypeStruct((NMOM, *TILE), F32),
        in_specs=[hbm] * 4,
        out_specs=pl.BlockSpec(memory_space=pltpu.VMEM),
        scratch_shapes=[
            pltpu.VMEM(vectors.shape, F32),
            pltpu.VMEM(positions.shape, F32),
            pltpu.VMEM(onsite.shape, F32),
            pltpu.VMEM(neighbors.shape, jnp.int32),
            tiles(3), tiles(4), pltpu.VMEM((4, *TILE), jnp.int32), pltpu.VMEM((4, *TILE), jnp.int32),
            tiles(5, 8), tiles(4, rows), tiles(4, rows), tiles(4, rows),
            tiles(rows), tiles(rows), tiles(rows),
            pltpu.VMEM((2, rows + 3, LANES), F32),
            pltpu.VMEM((3, 2, 2 * rows, LANES), F32),
            pltpu.VMEM((2, rows + 3, LANES), F32),
            pltpu.VMEM((3, 2, 2 * rows, LANES), F32),
            tiles(NMOM, NMOM), tiles(ntile - 1, NMOM),
            pltpu.SemaphoreType.DMA((4,)),
            pltpu.SemaphoreType.DMA((NMOM, 2)),
            pltpu.SemaphoreType.DMA((NMOM, 2)),
            pltpu.SemaphoreType.DMA((ntile - 1,)),
            pltpu.SemaphoreType.DMA((ntile - 1,)),
        ],
        compiler_params=pltpu.CompilerParams(
            collective_id=0, has_side_effects=True, vmem_limit_bytes=16 * 1024 * 1024
        ),
        cost_estimate=pl.CostEstimate(flops=10_000_000, bytes_accessed=150_000, transcendentals=10_000),
    )(vectors, positions, onsite, neighbors)
    return result.reshape(NMOM, GROUPS * LANES)


def solution(mesh):
    import functools
    in_specs = (P(None, "tile", "dom"), P(None, "dom"), P(None, "dom"), P(None, "dom"))
    out_specs = P("tile", "dom")
    local = functools.partial(body, mesh.shape["dom"], mesh.shape["tile"])
    return jax.shard_map(local, mesh=mesh, in_specs=in_specs, out_specs=out_specs, check_vma=False)
```

time: 347 us -> 37.5 us (0.11)
  the two profiles are of different devices: /device:TPU:2 before, /device:TPU:8 now
where the time goes in v1:
time: 37.5 us; the launch traced here: 37.2 us
  Pallas kernels  33.6 us (90%)
  local copies, waits for them, and re-layouts  3.6 us (10%)
    pallas_call x1, Pallas kernels, body(): pl.pallas_call(functools.partial(kernel, ndom, ntile), out_shape=jax.Shap...  33.6 us
    unnamed x9, local copies, waits for them, and re-layouts  3.6 us

profile of v1, /device:TPU:8, one launch (start us, length us, event | category | flops | bytes accessed | tf_op | source)
XLA Modules:
  0.0 37.2 jit_solution(11884389081925220914)
XLA Ops:
  0.0 0.0 copy-start
  0.0 0.8 %copy-done = f32[4,4,1024]{2,1,0:T(4,128)S(1)} copy-done((f32[4,4,1024]{2,1,0:T(4,128)S(1)}, f32[4,4,1024]{2,1,0:T(4,128)}, u32[]{:S(2)}) %copy-start) | copy-done | bytes 65560
  0.8 0.0 copy-start.1
  0.8 0.7 %copy-done.1 = f32[3,1024]{1,0:T(4,128)S(1)} copy-done((f32[3,1024]{1,0:T(4,128)S(1)}, f32[3,1024]{1,0:T(4,128)}, u32[]{:S(2)}) %copy-start.1) | copy-done | bytes 12312
  1.6 0.0 copy-start.2
  1.6 0.7 %copy-done.2 = f32[4,1024]{1,0:T(4,128)S(1)} copy-done((f32[4,1024]{1,0:T(4,128)S(1)}, f32[4,1024]{1,0:T(4,128)}, u32[]{:S(2)}) %copy-start.2) | copy-done | bytes 16408
  2.3 0.0 copy-start.3
  2.3 0.7 %copy-done.3 = s32[4,1024]{1,0:T(4,128)S(1)} copy-done((s32[4,1024]{1,0:T(4,128)S(1)}, s32[4,1024]{1,0:T(4,128)}, u32[]{:S(2)}) %copy-start.3) | copy-done | bytes 16408
  3.0 33.6 %shard_map.46 = f32[4,8,128]{2,1,0:T(8,128)S(1)} custom-call(f32[4,4,1024]{2,1,0:T(4,128)S(1)} %copy-done, f32[3,1024]{1,0:T(4,128)S(1)} %copy-done.1, f32[4,1024]{1,0:T(4,128)S(1)} %copy-done.2, s32[4,1024]{1,0:T(4,128)S(1)} %copy-done.3), custom_call_target="tpu_custom_call" | custom-call | flops 10000000 | bytes 150000 | tf_op jit(solution)/shard_map/pallas_call | solution.py:260
  36.6 0.6 %copy.7 = f32[1,4,8,128]{3,1,2,0:T(4,128)} copy(f32[1,4,8,128]{3,2,1,0:T(8,128)S(1)} %bitcast.4) | data formatting | bytes 32768
Async XLA Ops:
  0.0 0.8 %copy-start = (f32[4,4,1024]{2,1,0:T(4,128)S(1)}, f32[4,4,1024]{2,1,0:T(4,128)}, u32[]{:S(2)}) copy-start(f32[4,4,1024]{2,1,0:T(4,128)} %vec_hbm.1) | copy-start | bytes 196612
  0.8 0.7 %copy-start.1 = (f32[3,1024]{1,0:T(4,128)S(1)}, f32[3,1024]{1,0:T(4,128)}, u32[]{:S(2)}) copy-start(f32[3,1024]{1,0:T(4,128)} %pos_hbm.1) | copy-start | bytes 36868
  1.6 0.7 %copy-start.2 = (f32[4,1024]{1,0:T(4,128)S(1)}, f32[4,1024]{1,0:T(4,128)}, u32[]{:S(2)}) copy-start(f32[4,1024]{1,0:T(4,128)} %ons_hbm.1) | copy-start | bytes 49156
  2.3 0.7 %copy-start.3 = (s32[4,1024]{1,0:T(4,128)S(1)}, s32[4,1024]{1,0:T(4,128)}, u32[]{:S(2)}) copy-start(s32[4,1024]{1,0:T(4,128)} %nei_hbm.1) | copy-start | bytes 49156

commit v2 on v1

v2 whole, which is shorter than its diff:
```python
import jax
import jax.numpy as jnp
from jax import lax
from jax.experimental import pallas as pl
from jax.experimental.pallas import tpu as pltpu
from jax.sharding import PartitionSpec as P

BND = 128
VECS = 16
NMOM = 4
NORB = 4
LANES = 128
GROUPS = 8

onsite_s = -4.2
onsite_p = 1.72
hop_ss = -2.08
hop_sp = 2.48
hop_pps = 2.72
hop_ppp = -0.72
bond_length = 2.35
energy_scale = 16.0
length_scale = 2.0

MESH = pl.DeviceIdType.MESH
F32 = jnp.float32
TILE = (GROUPS, LANES)
POS, DIAG, CODE = 16, 19, 23
UNROLL = True


def lanes_of(source, index):
    return jnp.take_along_axis(source, index, axis=1, mode="promise_in_bounds")


def pick(bits, options):
    for bit in bits:
        options = [jnp.where(bit, options[i + 1], options[i]) for i in range(0, len(options), 2)]
    return options[0]


def kernel(
    ndom, ntile,
    vec_hbm, pos_hbm, ons_hbm, nei_hbm, out_ref,
    vec_in, pos_in, ons_in, nei_in,
    pos, diag, code, low, geo, a_all, b_all, c_all, h_a, h_b, k_a,
    send0, send, ghost0, ghost, local, whole_pos, whole_a, whole_b, strip, mom, mom_in,
    in_sem, halo_send, halo_recv, whole_send, whole_recv, mom_send, mom_recv,
):
    dom, tile = lax.axis_index("dom"), lax.axis_index("tile")
    up, down = lax.rem(dom + 1, ndom), lax.rem(dom + ndom - 1, ndom)

    barrier = pltpu.get_barrier_semaphore()
    for other in (up, down):
        pl.semaphore_signal(barrier, inc=1, device_id={"dom": other}, device_id_type=MESH)
    for step in range(1, ntile):
        peer = lax.rem(tile + step, ntile)
        pl.semaphore_signal(barrier, inc=1, device_id={"tile": peer}, device_id_type=MESH)

    loads = [
        pltpu.make_async_copy(source, target, in_sem.at[i])
        for i, (source, target) in enumerate(
            ((vec_hbm, vec_in), (pos_hbm, pos_in), (nei_hbm, nei_in), (ons_hbm, ons_in))
        )
    ]
    for load in loads:
        load.start()
    for load in loads:
        load.wait()

    for group in range(GROUPS):
        cut = pl.ds(group * LANES, LANES)
        for orbital in range(NORB):
            a_all[0, pl.ds(orbital * 4, 4), group, :] = vec_in[orbital, :, cut]
        pos[:, group, :] = pos_in[:, cut]
        diag[:, group, :] = ons_in[:, cut]
        code[:, group, :] = nei_in[:, cut]
    for orbital in range(NORB):
        base = onsite_s if orbital == 0 else onsite_p
        diag[orbital] = (base + diag[orbital]) / energy_scale
    for side, group in ((0, 0), (1, GROUPS - 1)):
        cut = pl.ds(group * LANES, LANES)
        for orbital in range(NORB):
            send0[side, pl.ds(orbital * 4, 4), :] = vec_in[orbital, :, cut]
        send0[side, pl.ds(POS, 3), :] = pos_in[:, cut]
        send0[side, pl.ds(DIAG, 4), :] = diag[:, group, :]
        send0[side, pl.ds(CODE, 4), :] = nei_in[:, cut].astype(F32)

    def both_ways(sources, target, send_sem, recv_sem):
        return [
            pltpu.make_async_remote_copy(
                src_ref=sources[side], dst_ref=target.at[1 - side],
                send_sem=send_sem.at[side], recv_sem=recv_sem.at[1 - side],
                device_id={"dom": other}, device_id_type=MESH,
            )
            for side, other in ((0, down), (1, up))
        ]

    ends = [
        both_ways((send0.at[0], send0.at[1]), ghost0, halo_send.at[0], halo_recv.at[0]),
        both_ways((send.at[0], send.at[1]), ghost, halo_send.at[1], halo_recv.at[1]),
    ]
    wholes = [
        both_ways((pos, pos), whole_pos, whole_send.at[0], whole_recv.at[0])
        + both_ways((a_all.at[0],) * 2, whole_a.at[0], whole_send.at[1], whole_recv.at[1]),
        both_ways((a_all.at[2],) * 2, whole_a.at[1], whole_send.at[2], whole_recv.at[2])
        + both_ways((b_all.at[1],) * 2, whole_b, whole_send.at[3], whole_recv.at[3]),
    ]

    pl.semaphore_wait(barrier, 2 + ntile - 1)
    for copy in ends[0] + wholes[0]:
        copy.start()

    for bond in range(4):
        low[bond] = jnp.bitwise_and(code[bond], LANES - 1)
        code[bond] = lax.shift_right_logical(code[bond], 7) - 1

    def gather(bond, ref, *row):
        bits = [jnp.bitwise_and(code[bond], 1 << bit) != 0 for bit in range(3)]
        return pick(bits, [
            lanes_of(jnp.broadcast_to(ref[(*row, pl.ds(group, 1), slice(None))], TILE), low[bond])
            for group in range(GROUPS)
        ])

    upper_half = lax.broadcasted_iota(jnp.int32, TILE, 0) >= GROUPS // 2

    def halves(below, above):
        return jnp.where(upper_half, jnp.broadcast_to(above, TILE), jnp.broadcast_to(below, TILE))

    def ends_of(ref, row):
        return halves(ref[0, pl.ds(row, 1), :], ref[1, pl.ds(row, 1), :])

    def gather_ghost(ref, row):
        return lanes_of(ends_of(ref, row), low[0])

    def put_geometry(slot, center, partner, bonded):
        offset = [partner[axis] - center[axis] for axis in range(3)]
        distance = jnp.sqrt(offset[0] * offset[0] + offset[1] * offset[1] + offset[2] * offset[2])
        away = distance - bond_length
        radial = jnp.where(bonded, jnp.exp(-0.5 * away * away) / energy_scale, 0.0)
        inverse = 1.0 / jnp.maximum(distance, 1.0)
        geo[slot, 0] = hop_ss * radial
        geo[slot, 1] = hop_sp * radial
        geo[slot, 2] = (hop_pps - hop_ppp) * radial
        geo[slot, 3] = hop_ppp * radial
        for axis in range(3):
            geo[slot, 4 + axis] = offset[axis] * inverse
        geo[slot, 7] = offset[0] * (-1.0 / length_scale)

    def hop(slot, beside):
        along = geo[slot, 4] * beside[1] + geo[slot, 5] * beside[2] + geo[slot, 6] * beside[3]
        mixed = geo[slot, 2] * along - geo[slot, 1] * beside[0]
        result = [geo[slot, 0] * beside[0] + geo[slot, 1] * along]
        for axis in range(3):
            result.append(geo[slot, 4 + axis] * mixed + geo[slot, 3] * beside[1 + axis])
        return result

    own_pos = [pos[axis] for axis in range(3)]
    for bond in range(4):
        inside = jnp.logical_and(code[bond] >= 0, code[bond] < GROUPS)
        put_geometry(bond, own_pos, [gather(bond, pos, axis) for axis in range(3)], inside)

    def gather_strip(beside, own, row):
        group = strip[1]
        bits = [jnp.bitwise_and(group, 1 << bit) != 0 for bit in range(3)]
        index = strip[0]
        inside = pick(bits, [
            lanes_of(halves(beside[0, row, pl.ds(g, 1), :], beside[1, row, pl.ds(g, 1), :]), index)
            for g in range(GROUPS)
        ])
        mine = lanes_of(halves(own[row, pl.ds(0, 1), :], own[row, pl.ds(GROUPS - 1, 1), :]), index)
        return jnp.where(jnp.logical_or(group == -1, group == GROUPS), mine, inside)

    def bond_sum(value):
        value = value + pltpu.roll(value, 1, 0)
        return value + pltpu.roll(value, 2, 0)

    def put_ends(slot, row, value):
        local[slot, 0, pl.ds(row, 1), :] = value[3:4]
        local[slot, 1, pl.ds(row, 1), :] = value[7:8]

    def strips_first():
        for side in range(2):
            strip[0, pl.ds(side * 4, 4), :] = ghost0[side, pl.ds(CODE, 4), :].astype(jnp.int32)
        number = strip[0]
        group = lax.shift_right_logical(number, 7) - 1
        strip[0] = jnp.bitwise_and(number, LANES - 1)
        strip[1] = group
        center = [ends_of(ghost0, POS + axis) for axis in range(3)]
        put_geometry(5, center, [gather_strip(whole_pos, pos, axis) for axis in range(3)], group < GROUPS + 1)

        def one(vector, carry):
            rows = [orbital * 4 + vector for orbital in range(NORB)]
            term = hop(5, [gather_strip(whole_a.at[0], a_all.at[0], row) for row in rows])
            for orbital, row in enumerate(rows):
                put_ends(0, row, ends_of(ghost0, DIAG + orbital) * ends_of(ghost0, row) + bond_sum(term[orbital]))
                put_ends(0, 16 + row, bond_sum(geo[5, 7] * term[orbital]))
            return carry

        lax.fori_loop(0, 4, one, 0, unroll=UNROLL)

    def strips_second():
        def one(vector, carry):
            rows = [orbital * 4 + vector for orbital in range(NORB)]
            for beside, own, shift in ((whole_a.at[1], a_all.at[2], 0), (whole_b, b_all.at[1], 16)):
                term = hop(5, [gather_strip(beside, own, row) for row in rows])
                for orbital, row in enumerate(rows):
                    value = ends_of(ghost0, DIAG + orbital) * ends_of(ghost, shift + row) + bond_sum(term[orbital])
                    put_ends(1, shift + row, 2.0 * value - ends_of(local.at[0], shift + row))
            return carry

        lax.fori_loop(0, 4, one, 0, unroll=UNROLL)

    for step in range(NMOM):
        has_b, last = step > 0, step == NMOM - 1

        def inner(vector, carry):
            rows = [orbital * 4 + vector for orbital in range(NORB)]
            h_sum, k_sum, hb_sum = [None] * NORB, [None] * NORB, [None] * NORB
            for bond in range(4):
                term = hop(bond, [gather(bond, a_all, step, row) for row in rows])
                drift = geo[bond, 7]
                for orbital in range(NORB):
                    moved = drift * term[orbital]
                    h_sum[orbital] = term[orbital] if bond == 0 else h_sum[orbital] + term[orbital]
                    k_sum[orbital] = moved if bond == 0 else k_sum[orbital] + moved
                if has_b:
                    term = hop(bond, [gather(bond, b_all, step - 1, row) for row in rows])
                    for orbital in range(NORB):
                        hb_sum[orbital] = term[orbital] if bond == 0 else hb_sum[orbital] + term[orbital]
            for orbital, row in enumerate(rows):
                k_a[row] = k_sum[orbital]
                if not last:
                    h_a[row] = h_sum[orbital]
                if has_b:
                    h_b[row] = hb_sum[orbital]
            return carry

        lax.fori_loop(0, 4, inner, 0)

        if step % 2 == 0:
            for copy in ends[step // 2]:
                copy.wait_recv()
            incoming = ghost if step else ghost0
        else:
            for copy in wholes[step // 2]:
                copy.wait_recv()
            (strips_second if step > 1 else strips_first)()
            incoming = local.at[step // 2]
        if step == 0:
            outside = jnp.logical_or(code[0] == -1, code[0] == GROUPS)
            put_geometry(4, own_pos, [gather_ghost(ghost0, POS + axis) for axis in range(3)], outside)

        def outer(vector, carry):
            rows = [orbital * 4 + vector for orbital in range(NORB)]
            term = hop(4, [gather_ghost(incoming, row) for row in rows])
            drift = geo[4, 7]
            for orbital, row in enumerate(rows):
                moved = k_a[row] + drift * term[orbital]
                if step == 0:
                    b_all[0, row] = moved
                c_all[step, row] = moved
                if not last:
                    value = diag[orbital] * a_all[step, row] + (h_a[row] + term[orbital])
                    if step > 0:
                        value = 2.0 * value - a_all[step - 1, row]
                    a_all[step + 1, row] = value
                    if step == 1:
                        send[0, pl.ds(row, 1), :] = value[0:1]
                        send[1, pl.ds(row, 1), :] = value[GROUPS - 1:]
            if has_b:
                term = hop(4, [gather_ghost(incoming, 16 + row) for row in rows])
                for orbital, row in enumerate(rows):
                    value = diag[orbital] * b_all[step - 1, row] + (h_b[row] + term[orbital])
                    if step > 1:
                        value = 2.0 * value - b_all[step - 2, row]
                    b_all[step, row] = value
                    if step == 1:
                        send[0, pl.ds(16 + row, 1), :] = value[0:1]
                        send[1, pl.ds(16 + row, 1), :] = value[GROUPS - 1:]
            return carry

        lax.fori_loop(0, 4, outer, 0, unroll=UNROLL)
        if step == 1:
            for copy in ends[1] + wholes[1]:
                copy.start()

        pairs = [(step, m) for m in range(step + 1)] + [(n, step) for n in range(step)]

        def moments(row, sums):
            b_rows = [b_all[n, row] for n in range(step + 1)]
            c_rows = [c_all[m, row] for m in range(step + 1)]
            return tuple(total + b_rows[n] * c_rows[m] for total, (n, m) in zip(sums, pairs))

        sums = lax.fori_loop(0, 16, moments, tuple(jnp.zeros(TILE, F32) for _ in pairs))
        for (n, m), total in zip(pairs, sums):
            mom[n, m] = total

    copies = []
    for step in range(1, ntile):
        peer = lax.rem(tile + step, ntile)
        copies.append(pltpu.make_async_remote_copy(
            src_ref=mom.at[peer], dst_ref=mom_in.at[step - 1],
            send_sem=mom_send.at[step - 1], recv_sem=mom_recv.at[step - 1],
            device_id={"tile": peer}, device_id_type=MESH,
        ))
    for copy in copies:
        copy.start()
    for copy in copies:
        copy.wait_recv()
    for m in range(NMOM):
        total = mom[tile, m]
        for other in range(ntile - 1):
            total = total + mom_in[other, m]
        out_ref[m] = total * (-1.0 / VECS)
    for group in ends + wholes + [copies]:
        for copy in group:
            copy.wait_send()


def body(ndom, ntile, vectors, positions, onsite, neighbors):
    import functools
    rows = NORB * vectors.shape[1]
    hbm = pl.BlockSpec(memory_space=pltpu.HBM)
    tiles = lambda *lead: pltpu.VMEM((*lead, *TILE), F32)
    result = pl.pallas_call(
        functools.partial(kernel, ndom, ntile),
        out_shape=jax.ShapeDtypeStruct((NMOM, *TILE), F32),
        in_specs=[hbm] * 4,
        out_specs=pl.BlockSpec(memory_space=pltpu.VMEM),
        scratch_shapes=[
            pltpu.VMEM(vectors.shape, F32),
            pltpu.VMEM(positions.shape, F32),
            pltpu.VMEM(onsite.shape, F32),
            pltpu.VMEM(neighbors.shape, jnp.int32),
            tiles(3), tiles(4), pltpu.VMEM((4, *TILE), jnp.int32), pltpu.VMEM((4, *TILE), jnp.int32),
            tiles(6, 8), tiles(4, rows), tiles(4, rows), tiles(4, rows),
            tiles(rows), tiles(rows), tiles(rows),
            pltpu.VMEM((2, CODE + 4, LANES), F32),
            pltpu.VMEM((2, 2 * rows, LANES), F32),
            pltpu.VMEM((2, CODE + 4, LANES), F32),
            pltpu.VMEM((2, 2 * rows, LANES), F32),
            pltpu.VMEM((2, 2, 2 * rows, LANES), F32),
            tiles(2, 3), tiles(2, 2, rows), tiles(2, rows),
            pltpu.VMEM((2, *TILE), jnp.int32),
            tiles(NMOM, NMOM), tiles(ntile - 1, NMOM),
            pltpu.SemaphoreType.DMA((4,)),
            pltpu.SemaphoreType.DMA((2, 2)),
            pltpu.SemaphoreType.DMA((2, 2)),
            pltpu.SemaphoreType.DMA((4, 2)),
            pltpu.SemaphoreType.DMA((4, 2)),
            pltpu.SemaphoreType.DMA((ntile - 1,)),
            pltpu.SemaphoreType.DMA((ntile - 1,)),
        ],
        compiler_params=pltpu.CompilerParams(
            collective_id=0, has_side_effects=True, vmem_limit_bytes=60 * 1024 * 1024
        ),
        cost_estimate=pl.CostEstimate(flops=10_000_000, bytes_accessed=150_000, transcendentals=10_000),
    )(vectors, positions, onsite, neighbors)
    return result.reshape(NMOM, GROUPS * LANES)


def solution(mesh):
    import functools
    in_specs = (P(None, "tile", "dom"), P(None, "dom"), P(None, "dom"), P(None, "dom"))
    out_specs = P("tile", "dom")
    local = functools.partial(body, mesh.shape["dom"], mesh.shape["tile"])
    return jax.shard_map(local, mesh=mesh, in_specs=in_specs, out_specs=out_specs, check_vma=False)
```

time: 37.5 us -> 30.7 us (0.82)
  Pallas kernels: 33.6 us -> 29.1 us
  local copies, waits for them, and re-layouts: 3.6 us -> 1.33 us
    pallas_call x1, Pallas kernels: 33.6 us -> 29.1 us  [body(): pl.pallas_call(functools.partial(kernel, ndom, ntile), out_shape=jax.Shap...]
    unnamed x9 -> x1, local copies, waits for them, and re-layouts: 3.6 us -> 1.33 us
where the time goes in v2:
time: 30.7 us; the launch traced here: 30.5 us
  Pallas kernels  29.1 us (95%)
  local copies, waits for them, and re-layouts  1.33 us (4%)
    pallas_call x1, Pallas kernels, body(): pl.pallas_call(functools.partial(kernel, ndom, ntile), out_shape=jax.Shap...  29.1 us
    unnamed x1, local copies, waits for them, and re-layouts  1.33 us

profile of v2, /device:TPU:8, one launch (start us, length us, event | category | flops | bytes accessed | tf_op | source)
XLA Modules:
  0.0 30.5 jit_solution(6786730881334852478)
XLA Ops:
  0.0 29.1 %shard_map.46 = f32[4,8,128]{2,1,0:T(8,128)} custom-call(f32[4,4,1024]{2,1,0:T(4,128)} %vec_hbm.1, f32[3,1024]{1,0:T(4,128)} %pos_hbm.1, f32[4,1024]{1,0:T(4,128)} %ons_hbm.1, s32[4,1024]{1,0:T(4,128)} %nei_hbm.1), custom_call_target="tpu_custom_call" | custom-call | flops 10000000 | bytes 150000 | tf_op jit(solution)/shard_map/pallas_call | solution.py:326
  29.1 1.3 %copy.7 = f32[1,4,8,128]{3,1,2,0:T(4,128)} copy(f32[1,4,8,128]{3,2,1,0:T(8,128)} %bitcast.4) | data formatting | bytes 32768

commit v3 on v1

v3 whole, which is shorter than its diff:
```python
import jax
import jax.numpy as jnp
from jax import lax
from jax.experimental import pallas as pl
from jax.experimental.pallas import tpu as pltpu
from jax.sharding import PartitionSpec as P

BND = 128
VECS = 16
NMOM = 4
NORB = 4
LANES = 128
GROUPS = 8

onsite_s = -4.2
onsite_p = 1.72
hop_ss = -2.08
hop_sp = 2.48
hop_pps = 2.72
hop_ppp = -0.72
bond_length = 2.35
energy_scale = 16.0
length_scale = 2.0

MESH = pl.DeviceIdType.MESH
F32 = jnp.float32
TILE = (GROUPS, LANES)
POS, CODE = 16, 19


def lanes_of(source, index):
    return jnp.take_along_axis(source, index, axis=1, mode="promise_in_bounds")


def pick(bits, options):
    for bit in bits:
        options = [jnp.where(bit, options[i + 1], options[i]) for i in range(0, len(options), 2)]
    return options[0]


def kernel(
    ndom, ntile,
    vec_hbm, pos_hbm, ons_hbm, nei_hbm, out_ref,
    vec_in, pos_in, ons_in, nei_in,
    pos, diag, code, low, geo, a_all, b_all, c_all, h_a, h_b, k_a, change, tip,
    send0, send, ghost0, ghost, mom, mom_in,
    in_sem, halo_send, halo_recv, mom_send, mom_recv,
):
    dom, tile = lax.axis_index("dom"), lax.axis_index("tile")
    up, down = lax.rem(dom + 1, ndom), lax.rem(dom + ndom - 1, ndom)

    barrier = pltpu.get_barrier_semaphore()
    for other in (up, down):
        pl.semaphore_signal(barrier, inc=1, device_id={"dom": other}, device_id_type=MESH)
    for step in range(1, ntile):
        peer = lax.rem(tile + step, ntile)
        pl.semaphore_signal(barrier, inc=1, device_id={"tile": peer}, device_id_type=MESH)

    loads = [
        pltpu.make_async_copy(source, target, in_sem.at[i])
        for i, (source, target) in enumerate(
            ((vec_hbm, vec_in), (pos_hbm, pos_in), (nei_hbm, nei_in), (ons_hbm, ons_in))
        )
    ]
    for load in loads:
        load.start()
    for load in loads:
        load.wait()

    for group in range(GROUPS):
        cut = pl.ds(group * LANES, LANES)
        for orbital in range(NORB):
            a_all[0, pl.ds(orbital * 4, 4), group, :] = vec_in[orbital, :, cut]
        pos[:, group, :] = pos_in[:, cut]
        diag[:, group, :] = ons_in[:, cut]
        code[:, group, :] = nei_in[:, cut]
    for orbital in range(NORB):
        base = onsite_s if orbital == 0 else onsite_p
        diag[orbital] = (base + diag[orbital]) / energy_scale
    for side, group in ((0, 0), (1, GROUPS - 1)):
        cut = pl.ds(group * LANES, LANES)
        for orbital in range(NORB):
            send0[side, pl.ds(orbital * 4, 4), :] = vec_in[orbital, :, cut]
        send0[side, pl.ds(POS, 3), :] = pos_in[:, cut]
        send0[side, pl.ds(CODE, 1), :] = nei_in[0:1, cut].astype(F32)

    def both_ways(sources, target, send_sem, recv_sem):
        return [
            pltpu.make_async_remote_copy(
                src_ref=sources[side], dst_ref=target.at[1 - side],
                send_sem=send_sem.at[side], recv_sem=recv_sem.at[1 - side],
                device_id={"dom": other}, device_id_type=MESH,
            )
            for side, other in ((0, down), (1, up))
        ]

    halos = [both_ways((send0.at[0], send0.at[1]), ghost0, halo_send.at[0], halo_recv.at[0])] + [
        both_ways((send.at[i, 0], send.at[i, 1]), ghost.at[i], halo_send.at[i + 1], halo_recv.at[i + 1])
        for i in range(3)
    ]

    pl.semaphore_wait(barrier, 2 + ntile - 1)
    for copy in halos[0]:
        copy.start()

    for bond in range(4):
        low[bond] = jnp.bitwise_and(code[bond], LANES - 1)
        code[bond] = lax.shift_right_logical(code[bond], 7) - 1

    def gather(bond, ref, *row):
        bits = [jnp.bitwise_and(code[bond], 1 << bit) != 0 for bit in range(3)]
        return pick(bits, [
            lanes_of(jnp.broadcast_to(ref[(*row, pl.ds(group, 1), slice(None))], TILE), low[bond])
            for group in range(GROUPS)
        ])

    upper_half = lax.broadcasted_iota(jnp.int32, TILE, 0) >= GROUPS // 2

    def halves(below, above):
        return jnp.where(upper_half, jnp.broadcast_to(above, TILE), jnp.broadcast_to(below, TILE))

    def ends_of(ref, row):
        return halves(ref[0, pl.ds(row, 1), :], ref[1, pl.ds(row, 1), :])

    def gather_ghost(ref, row):
        return lanes_of(ends_of(ref, row), low[0])

    def put_geometry(slot, center, partner, bonded):
        offset = [partner[axis] - center[axis] for axis in range(3)]
        distance = jnp.sqrt(offset[0] * offset[0] + offset[1] * offset[1] + offset[2] * offset[2])
        away = distance - bond_length
        radial = jnp.where(bonded, jnp.exp(-0.5 * away * away) / energy_scale, 0.0)
        inverse = 1.0 / jnp.maximum(distance, 1.0)
        geo[slot, 0] = hop_ss * radial
        geo[slot, 1] = hop_sp * radial
        geo[slot, 2] = (hop_pps - hop_ppp) * radial
        geo[slot, 3] = hop_ppp * radial
        for axis in range(3):
            geo[slot, 4 + axis] = offset[axis] * inverse
        geo[slot, 7] = offset[0] * (-1.0 / length_scale)

    def hop(slot, beside):
        along = geo[slot, 4] * beside[1] + geo[slot, 5] * beside[2] + geo[slot, 6] * beside[3]
        mixed = geo[slot, 2] * along - geo[slot, 1] * beside[0]
        result = [geo[slot, 0] * beside[0] + geo[slot, 1] * along]
        for axis in range(3):
            result.append(geo[slot, 4 + axis] * mixed + geo[slot, 3] * beside[1 + axis])
        return result

    own_pos = [pos[axis] for axis in range(3)]
    for bond in range(4):
        inside = jnp.logical_and(code[bond] >= 0, code[bond] < GROUPS)
        put_geometry(bond, own_pos, [gather(bond, pos, axis) for axis in range(3)], inside)

    def rows_of(vector):
        return [orbital * 4 + vector for orbital in range(NORB)]

    def add(total, term):
        return term if total is None else [x + y for x, y in zip(total, term)]

    def put_ends(slot, row, value):
        send[slot, 0, pl.ds(row, 1), :] = value[0:1]
        send[slot, 1, pl.ds(row, 1), :] = value[GROUPS - 1:]

    def interior(found, want_h, want_k):
        h_sum = k_sum = None
        for bond in range(4):
            term = hop(bond, found(bond))
            if want_h:
                h_sum = add(h_sum, term)
            if want_k:
                drift = geo[bond, 7]
                k_sum = add(k_sum, [drift * x for x in term])
        return h_sum, k_sum

    def gather_ends(bond, row):
        group, index = code[bond], low[bond]
        first = lanes_of(jnp.broadcast_to(change[row, pl.ds(0, 1), :], TILE), index)
        last = lanes_of(jnp.broadcast_to(change[row, pl.ds(GROUPS - 1, 1), :], TILE), index)
        return jnp.where(group == 0, first, jnp.where(group == GROUPS - 1, last, 0.0))

    def gather_mine(ref, row):
        return lanes_of(halves(ref[row, pl.ds(0, 1), :], ref[row, pl.ds(GROUPS - 1, 1), :]), low[4])

    def loop(function):
        lax.fori_loop(0, 4, lambda vector, carry: function(vector) or carry, 0)

    def loop_flat(function):
        for vector in range(4):
            function(vector)

    def moments_of(step):
        pairs = [(step, m) for m in range(step + 1)] + [(n, step) for n in range(step)]

        def moments(row, sums):
            b_rows = [b_all[n, row] for n in range(step + 1)]
            c_rows = [c_all[m, row] if m else b_rows[0] for m in range(step + 1)]
            return tuple(total + b_rows[n] * c_rows[m] for total, (n, m) in zip(sums, pairs))

        sums = lax.fori_loop(0, 16, moments, tuple(jnp.zeros(TILE, F32) for _ in pairs), unroll=4)
        for (n, m), total in zip(pairs, sums):
            mom[n, m] = total

    def first(vector):
        rows = rows_of(vector)
        h_sum, k_sum = interior(lambda bond: [gather(bond, a_all, 0, row) for row in rows], True, True)
        for orbital, row in enumerate(rows):
            value = diag[orbital] * a_all[0, row] + h_sum[orbital]
            a_all[1, row] = value
            b_all[0, row] = k_sum[orbital]
            put_ends(0, row, value)
            put_ends(0, 16 + row, k_sum[orbital])

    def second(vector):
        rows = rows_of(vector)
        h_sum, k_sum = interior(lambda bond: [gather(bond, a_all, 1, row) for row in rows], True, True)
        hb_sum, _ = interior(lambda bond: [gather(bond, b_all, 0, row) for row in rows], True, False)
        for orbital, row in enumerate(rows):
            h_a[row], k_a[row], h_b[row] = h_sum[orbital], k_sum[orbital], hb_sum[orbital]

    loop(first)
    for copy in halos[1]:
        copy.start()
    loop(second)

    for copy in halos[0]:
        copy.wait_recv()
    outside = jnp.logical_or(code[0] == -1, code[0] == GROUPS)
    put_geometry(4, own_pos, [gather_ghost(ghost0, POS + axis) for axis in range(3)], outside)
    number = ends_of(ghost0, CODE).astype(jnp.int32)
    group = lax.shift_right_logical(number, 7) - 1
    low[4] = jnp.bitwise_and(number, LANES - 1)
    put_geometry(
        5, [ends_of(ghost0, POS + axis) for axis in range(3)], [gather_mine(pos, axis) for axis in range(3)],
        jnp.logical_or(group == -1, group == GROUPS),
    )

    def third(vector):
        rows = rows_of(vector)
        term = hop(4, [gather_ghost(ghost0, row) for row in rows])
        mine = hop(5, [gather_mine(a_all.at[0], row) for row in rows])
        for orbital, row in enumerate(rows):
            moved = geo[4, 7] * term[orbital]
            change[row], change[16 + row] = term[orbital], moved
            a_all[1, row] = a_all[1, row] + term[orbital]
            b_all[0, row] = b_all[0, row] + moved
            tip[row], tip[16 + row] = mine[orbital], geo[5, 7] * mine[orbital]

    def fourth(vector):
        rows = rows_of(vector)
        h_sum, k_sum = interior(lambda bond: [gather_ends(bond, row) for row in rows], True, True)
        hb_sum, _ = interior(lambda bond: [gather_ends(bond, 16 + row) for row in rows], True, False)
        for orbital, row in enumerate(rows):
            h_a[row], k_a[row] = h_a[row] + h_sum[orbital], k_a[row] + k_sum[orbital]
            h_b[row] = h_b[row] + hb_sum[orbital]

    def ghost_terms(vector, slot):
        rows = rows_of(vector)
        return [
            hop(4, [lanes_of(tip[shift + row] + ends_of(ghost.at[slot], shift + row), low[0]) for row in rows])
            for shift in (0, 16)
        ]

    def fifth(vector):
        term, term_b = ghost_terms(vector, 0)
        for orbital, row in enumerate(rows_of(vector)):
            c_all[1, row] = k_a[row] + geo[4, 7] * term[orbital]
            value = 2.0 * (diag[orbital] * a_all[1, row] + (h_a[row] + term[orbital])) - a_all[0, row]
            value_b = diag[orbital] * b_all[0, row] + (h_b[row] + term_b[orbital])
            a_all[2, row], b_all[1, row] = value, value_b
            put_ends(1, row, value)
            put_ends(1, 16 + row, value_b)

    loop_flat(third)
    loop_flat(fourth)
    for copy in halos[1]:
        copy.wait_recv()
    loop_flat(fifth)
    for copy in halos[2]:
        copy.start()

    def sixth(vector):
        rows = rows_of(vector)
        h_sum, k_sum = interior(lambda bond: [gather(bond, a_all, 2, row) for row in rows], True, True)
        hb_sum, _ = interior(lambda bond: [gather(bond, b_all, 1, row) for row in rows], True, False)
        for orbital, row in enumerate(rows):
            value = 2.0 * (diag[orbital] * a_all[2, row] + h_sum[orbital]) - a_all[1, row]
            value_b = 2.0 * (diag[orbital] * b_all[1, row] + hb_sum[orbital]) - b_all[0, row]
            a_all[3, row], b_all[2, row], c_all[2, row] = value, value_b, k_sum[orbital]
            put_ends(2, row, value)
            put_ends(2, 16 + row, value_b)

    def seventh(vector):
        rows = rows_of(vector)
        _, k_sum = interior(lambda bond: [gather(bond, a_all, 3, row) for row in rows], False, True)
        hb_sum, _ = interior(lambda bond: [gather(bond, b_all, 2, row) for row in rows], True, False)
        mine = hop(5, [gather_mine(a_all.at[2], row) for row in rows])
        mine_b = hop(5, [gather_mine(b_all.at[1], row) for row in rows])
        for orbital, row in enumerate(rows):
            k_a[row], h_b[row] = k_sum[orbital], hb_sum[orbital]
            tip[row], tip[16 + row] = 2.0 * mine[orbital], 2.0 * mine_b[orbital]

    loop(sixth)
    for copy in halos[3]:
        copy.start()
    loop(seventh)
    moments_of(0)
    moments_of(1)

    for copy in halos[2]:
        copy.wait_recv()

    def eighth(vector):
        rows = rows_of(vector)
        term = hop(4, [gather_ghost(ghost.at[1], row) for row in rows])
        term_b = hop(4, [gather_ghost(ghost.at[1], 16 + row) for row in rows])
        for orbital, row in enumerate(rows):
            change[row], change[16 + row] = 2.0 * term[orbital], 2.0 * term_b[orbital]
            c_all[2, row] = c_all[2, row] + geo[4, 7] * term[orbital]
            b_all[2, row] = b_all[2, row] + 2.0 * term_b[orbital]

    def ninth(vector):
        rows = rows_of(vector)
        _, k_sum = interior(lambda bond: [gather_ends(bond, row) for row in rows], False, True)
        hb_sum, _ = interior(lambda bond: [gather_ends(bond, 16 + row) for row in rows], True, False)
        for orbital, row in enumerate(rows):
            k_a[row], h_b[row] = k_a[row] + k_sum[orbital], h_b[row] + hb_sum[orbital]

    def tenth(vector):
        term, term_b = ghost_terms(vector, 2)
        for orbital, row in enumerate(rows_of(vector)):
            c_all[3, row] = k_a[row] + geo[4, 7] * term[orbital]
            b_all[3, row] = 2.0 * (diag[orbital] * b_all[2, row] + (h_b[row] + term_b[orbital])) - b_all[1, row]

    loop_flat(eighth)
    loop_flat(ninth)
    moments_of(2)
    for copy in halos[3]:
        copy.wait_recv()
    loop_flat(tenth)
    moments_of(3)

    copies = []
    for step in range(1, ntile):
        peer = lax.rem(tile + step, ntile)
        copies.append(pltpu.make_async_remote_copy(
            src_ref=mom.at[peer], dst_ref=mom_in.at[step - 1],
            send_sem=mom_send.at[step - 1], recv_sem=mom_recv.at[step - 1],
            device_id={"tile": peer}, device_id_type=MESH,
        ))
    for copy in copies:
        copy.start()
    for copy in copies:
        copy.wait_recv()
    for m in range(NMOM):
        total = mom[tile, m]
        for other in range(ntile - 1):
            total = total + mom_in[other, m]
        out_ref[m] = total * (-1.0 / VECS)
    for group in halos + [copies]:
        for copy in group:
            copy.wait_send()


def body(ndom, ntile, vectors, positions, onsite, neighbors):
    import functools
    rows = NORB * vectors.shape[1]
    hbm = pl.BlockSpec(memory_space=pltpu.HBM)
    tiles = lambda *lead: pltpu.VMEM((*lead, *TILE), F32)
    result = pl.pallas_call(
        functools.partial(kernel, ndom, ntile),
        out_shape=jax.ShapeDtypeStruct((NMOM, *TILE), F32),
        in_specs=[hbm] * 4,
        out_specs=pl.BlockSpec(memory_space=pltpu.VMEM),
        scratch_shapes=[
            pltpu.VMEM(vectors.shape, F32),
            pltpu.VMEM(positions.shape, F32),
            pltpu.VMEM(onsite.shape, F32),
            pltpu.VMEM(neighbors.shape, jnp.int32),
            tiles(3), tiles(4), pltpu.VMEM((4, *TILE), jnp.int32), pltpu.VMEM((5, *TILE), jnp.int32),
            tiles(6, 8), tiles(4, rows), tiles(4, rows), tiles(4, rows),
            tiles(rows), tiles(rows), tiles(rows), tiles(2 * rows), tiles(2 * rows),
            pltpu.VMEM((2, CODE + 1, LANES), F32),
            pltpu.VMEM((3, 2, 2 * rows, LANES), F32),
            pltpu.VMEM((2, CODE + 1, LANES), F32),
            pltpu.VMEM((3, 2, 2 * rows, LANES), F32),
            tiles(NMOM, NMOM), tiles(ntile - 1, NMOM),
            pltpu.SemaphoreType.DMA((4,)),
            pltpu.SemaphoreType.DMA((4, 2)),
            pltpu.SemaphoreType.DMA((4, 2)),
            pltpu.SemaphoreType.DMA((ntile - 1,)),
            pltpu.SemaphoreType.DMA((ntile - 1,)),
        ],
        compiler_params=pltpu.CompilerParams(
            collective_id=0, has_side_effects=True, vmem_limit_bytes=60 * 1024 * 1024
        ),
        cost_estimate=pl.CostEstimate(flops=10_000_000, bytes_accessed=150_000, transcendentals=10_000),
    )(vectors, positions, onsite, neighbors)
    return result.reshape(NMOM, GROUPS * LANES)


def solution(mesh):
    import functools
    in_specs = (P(None, "tile", "dom"), P(None, "dom"), P(None, "dom"), P(None, "dom"))
    out_specs = P("tile", "dom")
    local = functools.partial(body, mesh.shape["dom"], mesh.shape["tile"])
    return jax.shard_map(local, mesh=mesh, in_specs=in_specs, out_specs=out_specs, check_vma=False)
```

time: 37.5 us -> 29.2 us (0.78)
  Pallas kernels: 33.6 us -> 27.6 us
  local copies, waits for them, and re-layouts: 3.6 us -> 1.33 us
    pallas_call x1, Pallas kernels: 33.6 us -> 27.6 us  [body(): pl.pallas_call(functools.partial(kernel, ndom, ntile), out_shape=jax.Shap...]
    unnamed x9 -> x1, local copies, waits for them, and re-layouts: 3.6 us -> 1.33 us
where the time goes in v3:
time: 29.2 us; the launch traced here: 28.9 us
  Pallas kernels  27.6 us (95%)
  local copies, waits for them, and re-layouts  1.33 us (5%)
    pallas_call x1, Pallas kernels, body(): pl.pallas_call(functools.partial(kernel, ndom, ntile), out_shape=jax.Shap...  27.6 us
    unnamed x1, local copies, waits for them, and re-layouts  1.33 us

profile of v3, /device:TPU:8, one launch (start us, length us, event | category | flops | bytes accessed | tf_op | source)
XLA Modules:
  0.0 28.9 jit_solution(7144651707346357225)
XLA Ops:
  0.0 27.6 %shard_map.46 = f32[4,8,128]{2,1,0:T(8,128)} custom-call(f32[4,4,1024]{2,1,0:T(4,128)} %vec_hbm.1, f32[3,1024]{1,0:T(4,128)} %pos_hbm.1, f32[4,1024]{1,0:T(4,128)} %ons_hbm.1, s32[4,1024]{1,0:T(4,128)} %nei_hbm.1), custom_call_target="tpu_custom_call" | custom-call | flops 10000000 | bytes 150000 | tf_op jit(solution)/shard_map/pallas_call | solution.py:370
  27.6 1.3 %copy.7 = f32[1,4,8,128]{3,1,2,0:T(4,128)} copy(f32[1,4,8,128]{3,2,1,0:T(8,128)} %bitcast.4) | data formatting | bytes 32768

commit v4 on v3

--- a/solution.py
+++ b/solution.py
@@ -72,8 +72,8 @@
         for orbital in range(NORB):
             a_all[0, pl.ds(orbital * 4, 4), group, :] = vec_in[orbital, :, cut]
         pos[:, group, :] = pos_in[:, cut]
-        diag[:, group, :] = ons_in[:, cut]
-        code[:, group, :] = nei_in[:, cut]
+        diag[pl.ds(0, 4), group, :] = ons_in[:, cut]
+        code[pl.ds(0, 4), group, :] = nei_in[:, cut]
     for orbital in range(NORB):
         base = onsite_s if orbital == 0 else onsite_p
         diag[orbital] = (base + diag[orbital]) / energy_scale
@@ -98,10 +98,6 @@
         both_ways((send.at[i, 0], send.at[i, 1]), ghost.at[i], halo_send.at[i + 1], halo_recv.at[i + 1])
         for i in range(3)
     ]
-
-    pl.semaphore_wait(barrier, 2 + ntile - 1)
-    for copy in halos[0]:
-        copy.start()
 
     for bond in range(4):
         low[bond] = jnp.bitwise_and(code[bond], LANES - 1)
@@ -152,6 +148,41 @@
         inside = jnp.logical_and(code[bond] >= 0, code[bond] < GROUPS)
         put_geometry(bond, own_pos, [gather(bond, pos, axis) for axis in range(3)], inside)
 
+    def put_own_ends():
+        for side, group in ((0, 0), (1, GROUPS - 1)):
+            for bond in range(4):
+                place = pl.ds(side * 4 + bond, 1)
+                low[5, place, :] = low[bond, pl.ds(group, 1), :]
+                code[4, place, :] = code[bond, pl.ds(group, 1), :]
+                for entry in range(7):
+                    geo[6, entry, place, :] = geo[bond, entry, pl.ds(group, 1), :]
+        for orbital in range(NORB):
+            diag[4 + orbital] = halves(diag[orbital, pl.ds(0, 1), :], diag[orbital, pl.ds(GROUPS - 1, 1), :])
+
+    def bond_sum(value):
+        value = value + pltpu.roll(value, 1, 0)
+        return value + pltpu.roll(value, 2, 0)
+
+    def own_ends(ref, row):
+        return halves(ref[row, pl.ds(0, 1), :], ref[row, pl.ds(GROUPS - 1, 1), :])
+
+    def next_ends(current, past, row_shift):
+        bits = [jnp.bitwise_and(code[4], 1 << bit) != 0 for bit in range(3)]
+        for vector in range(4):
+            rows = rows_of(vector)
+            term = hop(6, [
+                pick(bits, [
+                    lanes_of(jnp.broadcast_to(current[row, pl.ds(group, 1), :], TILE), low[5])
+                    for group in range(GROUPS)
+                ])
+                for row in rows
+            ])
+            for orbital, row in enumerate(rows):
+                value = diag[4 + orbital] * own_ends(current, row) + bond_sum(term[orbital])
+                value = 2.0 * value - own_ends(past, row)
+                send[2, 0, pl.ds(row_shift + row, 1), :] = value[3:4]
+                send[2, 1, pl.ds(row_shift + row, 1), :] = value[7:8]
+
     def rows_of(vector):
         return [orbital * 4 + vector for orbital in range(NORB)]
 
@@ -201,6 +232,20 @@
         for (n, m), total in zip(pairs, sums):
             mom[n, m] = total
 
+    def to_peer(step, part, rows):
+        peer = lax.rem(tile + step, ntile)
+        return pltpu.make_async_remote_copy(
+            src_ref=mom.at[peer, rows], dst_ref=mom_in.at[step - 1, rows],
+            send_sem=mom_send.at[part, step - 1], recv_sem=mom_recv.at[part, step - 1],
+            device_id={"tile": peer}, device_id_type=MESH,
+        )
+
+    others = range(1, ntile)
+    owns_last = [lax.rem(tile + step, ntile) == NMOM - 1 for step in others]
+    early = [to_peer(step, 0, pl.ds(0, NMOM - 1)) for step in others]
+    late_one = [to_peer(step, 1, pl.ds(NMOM - 1, 1)) for step in others]
+    late_all = [to_peer(step, 2, pl.ds(0, NMOM)) for step in others]
+
     def first(vector):
         rows = rows_of(vector)
         h_sum, k_sum = interior(lambda bond: [gather(bond, a_all, 0, row) for row in rows], True, True)
@@ -219,9 +264,11 @@
             h_a[row], k_a[row], h_b[row] = h_sum[orbital], k_sum[orbital], hb_sum[orbital]
 
     loop(first)
-    for copy in halos[1]:
+    pl.semaphore_wait(barrier, 2 + ntile - 1)
+    for copy in halos[0] + halos[1]:
         copy.start()
     loop(second)
+    put_own_ends()
 
     for copy in halos[0]:
         copy.wait_recv()
@@ -287,8 +334,6 @@
             value = 2.0 * (diag[orbital] * a_all[2, row] + h_sum[orbital]) - a_all[1, row]
             value_b = 2.0 * (diag[orbital] * b_all[1, row] + hb_sum[orbital]) - b_all[0, row]
             a_all[3, row], b_all[2, row], c_all[2, row] = value, value_b, k_sum[orbital]
-            put_ends(2, row, value)
-            put_ends(2, 16 + row, value_b)
 
     def seventh(vector):
         rows = rows_of(vector)
@@ -300,9 +345,11 @@
             k_a[row], h_b[row] = k_sum[orbital], hb_sum[orbital]
             tip[row], tip[16 + row] = 2.0 * mine[orbital], 2.0 * mine_b[orbital]
 
-    loop(sixth)
+    next_ends(a_all.at[2], a_all.at[1], 0)
+    next_ends(b_all.at[1], b_all.at[0], 16)
     for copy in halos[3]:
         copy.start()
+    loop(sixth)
     loop(seventh)
     moments_of(0)
     moments_of(1)
@@ -335,31 +382,33 @@
     loop_flat(eighth)
     loop_flat(ninth)
     moments_of(2)
+    for copy, only in zip(early, owns_last):
+        pl.when(jnp.logical_not(only))(copy.start)
     for copy in halos[3]:
         copy.wait_recv()
     loop_flat(tenth)
     moments_of(3)
 
-    copies = []
-    for step in range(1, ntile):
-        peer = lax.rem(tile + step, ntile)
-        copies.append(pltpu.make_async_remote_copy(
-            src_ref=mom.at[peer], dst_ref=mom_in.at[step - 1],
-            send_sem=mom_send.at[step - 1], recv_sem=mom_recv.at[step - 1],
-            device_id={"tile": peer}, device_id_type=MESH,
-        ))
-    for copy in copies:
-        copy.start()
-    for copy in copies:
-        copy.wait_recv()
+    for copy, only in zip(late_all, owns_last):
+        pl.when(only)(copy.start)
+    for copy, only in zip(late_one, owns_last):
+        pl.when(jnp.logical_not(only))(copy.start)
+    mine = tile == NMOM - 1
+    for copy in late_all:
+        pl.when(mine)(copy.wait_recv)
+    for copy in late_one + early:
+        pl.when(jnp.logical_not(mine))(copy.wait_recv)
     for m in range(NMOM):
         total = mom[tile, m]
         for other in range(ntile - 1):
             total = total + mom_in[other, m]
         out_ref[m] = total * (-1.0 / VECS)
-    for group in halos + [copies]:
+    for group in halos:
         for copy in group:
             copy.wait_send()
+    for copies, when in ((late_all, True), (late_one, False), (early, False)):
+        for copy, only in zip(copies, owns_last):
+            pl.when(only if when else jnp.logical_not(only))(copy.wait_send)
 
 
 def body(ndom, ntile, vectors, positions, onsite, neighbors):
@@ -377,8 +426,8 @@
             pltpu.VMEM(positions.shape, F32),
             pltpu.VMEM(onsite.shape, F32),
             pltpu.VMEM(neighbors.shape, jnp.int32),
-            tiles(3), tiles(4), pltpu.VMEM((4, *TILE), jnp.int32), pltpu.VMEM((5, *TILE), jnp.int32),
-            tiles(6, 8), tiles(4, rows), tiles(4, rows), tiles(4, rows),
+            tiles(3), tiles(8), pltpu.VMEM((5, *TILE), jnp.int32), pltpu.VMEM((6, *TILE), jnp.int32),
+            tiles(7, 8), tiles(4, rows), tiles(4, rows), tiles(4, rows),
             tiles(rows), tiles(rows), tiles(rows), tiles(2 * rows), tiles(2 * rows),
             pltpu.VMEM((2, CODE + 1, LANES), F32),
             pltpu.VMEM((3, 2, 2 * rows, LANES), F32),
@@ -388,14 +437,14 @@
             pltpu.SemaphoreType.DMA((4,)),
             pltpu.SemaphoreType.DMA((4, 2)),
             pltpu.SemaphoreType.DMA((4, 2)),
-            pltpu.SemaphoreType.DMA((ntile - 1,)),
-            pltpu.SemaphoreType.DMA((ntile - 1,)),
+            pltpu.SemaphoreType.DMA((3, ntile - 1)),
+            pltpu.SemaphoreType.DMA((3, ntile - 1)),
         ],
         compiler_params=pltpu.CompilerParams(
-            collective_id=0, has_side_effects=True, vmem_limit_bytes=60 * 1024 * 1024
+            collective_id=0, has_side_effects=True, vmem_limit_bytes=16 * 1024 * 1024
         ),
         cost_estimate=pl.CostEstimate(flops=10_000_000, bytes_accessed=150_000, transcendentals=10_000),
-    )(vectors, positions, onsite, neighbors)
+    )(*[pltpu.with_memory_space_constraint(x, pltpu.HBM) for x in (vectors, positions, onsite, neighbors)])
     return result.reshape(NMOM, GROUPS * LANES)
 
 

time: 29.2 us -> 26.3 us (0.901)
  Pallas kernels: 27.6 us -> 25.5 us
  local copies, waits for them, and re-layouts: 1.33 us -> 0.61 us
    pallas_call x1, Pallas kernels: 27.6 us -> 25.5 us  [body(): pl.pallas_call(functools.partial(kernel, ndom, ntile), out_shape=jax.Shap...]
    unnamed x1, local copies, waits for them, and re-layouts: 1.33 us -> 0.61 us
where the time goes in v4:
time: 26.3 us; the launch traced here: 26.1 us
  Pallas kernels  25.5 us (97%)
  local copies, waits for them, and re-layouts  0.61 us (2%)
    pallas_call x1, Pallas kernels, body(): pl.pallas_call(functools.partial(kernel, ndom, ntile), out_shape=jax.Shap...  25.5 us
    unnamed x1, local copies, waits for them, and re-layouts  0.61 us

profile of v4, /device:TPU:8, one launch (start us, length us, event | category | flops | bytes accessed | tf_op | source)
XLA Modules:
  0.0 26.1 jit_solution(4854406082890894267)
XLA Ops:
  0.0 25.5 %shard_map.46 = f32[4,8,128]{2,1,0:T(8,128)S(1)} custom-call(f32[4,4,1024]{2,1,0:T(4,128)} %vec_hbm.1, f32[3,1024]{1,0:T(4,128)} %pos_hbm.1, f32[4,1024]{1,0:T(4,128)} %ons_hbm.1, s32[4,1024]{1,0:T(4,128)} %nei_hbm.1), custom_call_target="tpu_custom_call" | custom-call | flops 10000000 | bytes 150000 | tf_op jit(solution)/shard_map/pallas_call | solution.py:419
  25.5 0.6 %copy.7 = f32[1,4,8,128]{3,1,2,0:T(4,128)} copy(f32[1,4,8,128]{3,2,1,0:T(8,128)S(1)} %bitcast.4) | data formatting | bytes 32768

commit v5 on v4

--- a/solution.py
+++ b/solution.py
@@ -204,11 +204,14 @@
                 k_sum = add(k_sum, [drift * x for x in term])
         return h_sum, k_sum
 
+    def ends_at(bond, first, last):
+        group, index = code[bond], low[bond]
+        first = lanes_of(jnp.broadcast_to(first, TILE), index)
+        last = lanes_of(jnp.broadcast_to(last, TILE), index)
+        return jnp.where(group == 0, first, jnp.where(group == GROUPS - 1, last, 0.0))
+
     def gather_ends(bond, row):
-        group, index = code[bond], low[bond]
-        first = lanes_of(jnp.broadcast_to(change[row, pl.ds(0, 1), :], TILE), index)
-        last = lanes_of(jnp.broadcast_to(change[row, pl.ds(GROUPS - 1, 1), :], TILE), index)
-        return jnp.where(group == 0, first, jnp.where(group == GROUPS - 1, last, 0.0))
+        return ends_at(bond, change[row, pl.ds(0, 1), :], change[row, pl.ds(GROUPS - 1, 1), :])
 
     def gather_mine(ref, row):
         return lanes_of(halves(ref[row, pl.ds(0, 1), :], ref[row, pl.ds(GROUPS - 1, 1), :]), low[4])
@@ -240,7 +243,7 @@
             device_id={"tile": peer}, device_id_type=MESH,
         )
 
-    others = range(1, ntile)
+    others = sorted(range(1, ntile), key=lambda step: -min(step, ntile - step))
     owns_last = [lax.rem(tile + step, ntile) == NMOM - 1 for step in others]
     early = [to_peer(step, 0, pl.ds(0, NMOM - 1)) for step in others]
     late_one = [to_peer(step, 1, pl.ds(NMOM - 1, 1)) for step in others]
@@ -288,18 +291,22 @@
         mine = hop(5, [gather_mine(a_all.at[0], row) for row in rows])
         for orbital, row in enumerate(rows):
             moved = geo[4, 7] * term[orbital]
-            change[row], change[16 + row] = term[orbital], moved
+            change[row] = term[orbital]
             a_all[1, row] = a_all[1, row] + term[orbital]
             b_all[0, row] = b_all[0, row] + moved
             tip[row], tip[16 + row] = mine[orbital], geo[5, 7] * mine[orbital]
 
-    def fourth(vector):
-        rows = rows_of(vector)
-        h_sum, k_sum = interior(lambda bond: [gather_ends(bond, row) for row in rows], True, True)
-        hb_sum, _ = interior(lambda bond: [gather_ends(bond, 16 + row) for row in rows], True, False)
-        for orbital, row in enumerate(rows):
-            h_a[row], k_a[row] = h_a[row] + h_sum[orbital], k_a[row] + k_sum[orbital]
-            h_b[row] = h_b[row] + hb_sum[orbital]
+    def fourth():
+        for bond in range(4):
+            drift = geo[bond, 7]
+            moved = ends_at(bond, geo[4, 7, pl.ds(0, 1), :], geo[4, 7, pl.ds(GROUPS - 1, 1), :])
+            for vector in range(4):
+                rows = rows_of(vector)
+                term = hop(bond, [gather_ends(bond, row) for row in rows])
+                for orbital, row in enumerate(rows):
+                    h_a[row] = h_a[row] + term[orbital]
+                    k_a[row] = k_a[row] + drift * term[orbital]
+                    h_b[row] = h_b[row] + moved * term[orbital]
 
     def ghost_terms(vector, slot):
         rows = rows_of(vector)
@@ -319,11 +326,11 @@
             put_ends(1, 16 + row, value_b)
 
     loop_flat(third)
-    loop_flat(fourth)
+    fourth()
     for copy in halos[1]:
         copy.wait_recv()
     loop_flat(fifth)
-    for copy in halos[2]:
+    for copy in halos[2][::-1]:
         copy.start()
 
     def sixth(vector):
@@ -347,7 +354,7 @@
 
     next_ends(a_all.at[2], a_all.at[1], 0)
     next_ends(b_all.at[1], b_all.at[0], 16)
-    for copy in halos[3]:
+    for copy in halos[3][::-1]:
         copy.start()
     loop(sixth)
     loop(seventh)
@@ -373,11 +380,22 @@
         for orbital, row in enumerate(rows):
             k_a[row], h_b[row] = k_a[row] + k_sum[orbital], h_b[row] + hb_sum[orbital]
 
-    def tenth(vector):
-        term, term_b = ghost_terms(vector, 2)
-        for orbital, row in enumerate(rows_of(vector)):
-            c_all[3, row] = k_a[row] + geo[4, 7] * term[orbital]
-            b_all[3, row] = 2.0 * (diag[orbital] * b_all[2, row] + (h_b[row] + term_b[orbital])) - b_all[1, row]
+    last_pairs = [(3, m) for m in range(4)] + [(n, 3) for n in range(3)]
+
+    def tenth():
+        sums = [None] * len(last_pairs)
+        for vector in range(4):
+            term, term_b = ghost_terms(vector, 2)
+            for orbital, row in enumerate(rows_of(vector)):
+                c_last = k_a[row] + geo[4, 7] * term[orbital]
+                b_last = 2.0 * (diag[orbital] * b_all[2, row] + (h_b[row] + term_b[orbital])) - b_all[1, row]
+                b_rows = [b_all[n, row] for n in range(3)] + [b_last]
+                c_rows = [b_rows[0], c_all[1, row], c_all[2, row], c_last]
+                for at, (n, m) in enumerate(last_pairs):
+                    part = b_rows[n] * c_rows[m]
+                    sums[at] = part if sums[at] is None else sums[at] + part
+        for (n, m), total in zip(last_pairs, sums):
+            mom[n, m] = total
 
     loop_flat(eighth)
     loop_flat(ninth)
@@ -386,8 +404,7 @@
         pl.when(jnp.logical_not(only))(copy.start)
     for copy in halos[3]:
         copy.wait_recv()
-    loop_flat(tenth)
-    moments_of(3)
+    tenth()
 
     for copy, only in zip(late_all, owns_last):
         pl.when(only)(copy.start)

time: 26.3 us -> 26.1 us (level)
  no operation moved by 1% of the time
where the time goes in v5:
time: 26.1 us; the launch traced here: 26 us
  Pallas kernels  25.4 us (97%)
  local copies, waits for them, and re-layouts  0.61 us (2%)
    pallas_call x1, Pallas kernels, body(): pl.pallas_call(functools.partial(kernel, ndom, ntile), out_shape=jax.Shap...  25.4 us
    unnamed x1, local copies, waits for them, and re-layouts  0.61 us

profile of v5, /device:TPU:8, one launch (start us, length us, event | category | flops | bytes accessed | tf_op | source)
XLA Modules:
  0.0 26.0 jit_solution(10551978735593955926)
XLA Ops:
  0.0 25.4 %shard_map.46 = f32[4,8,128]{2,1,0:T(8,128)S(1)} custom-call(f32[4,4,1024]{2,1,0:T(4,128)} %vec_hbm.1, f32[3,1024]{1,0:T(4,128)} %pos_hbm.1, f32[4,1024]{1,0:T(4,128)} %ons_hbm.1, s32[4,1024]{1,0:T(4,128)} %nei_hbm.1), custom_call_target="tpu_custom_call" | custom-call | flops 10000000 | bytes 150000 | tf_op jit(solution)/shard_map/pallas_call | solution.py:436
  25.4 0.6 %copy.7 = f32[1,4,8,128]{3,1,2,0:T(4,128)} copy(f32[1,4,8,128]{3,2,1,0:T(8,128)S(1)} %bitcast.4) | data formatting | bytes 32768

commit v6 on v5

--- a/solution.py
+++ b/solution.py
@@ -235,19 +235,16 @@
         for (n, m), total in zip(pairs, sums):
             mom[n, m] = total
 
-    def to_peer(step, part, rows):
+    def to_peer(step):
         peer = lax.rem(tile + step, ntile)
         return pltpu.make_async_remote_copy(
-            src_ref=mom.at[peer, rows], dst_ref=mom_in.at[step - 1, rows],
-            send_sem=mom_send.at[part, step - 1], recv_sem=mom_recv.at[part, step - 1],
+            src_ref=mom.at[peer], dst_ref=mom_in.at[step - 1],
+            send_sem=mom_send.at[step - 1], recv_sem=mom_recv.at[step - 1],
             device_id={"tile": peer}, device_id_type=MESH,
         )
 
     others = sorted(range(1, ntile), key=lambda step: -min(step, ntile - step))
-    owns_last = [lax.rem(tile + step, ntile) == NMOM - 1 for step in others]
-    early = [to_peer(step, 0, pl.ds(0, NMOM - 1)) for step in others]
-    late_one = [to_peer(step, 1, pl.ds(NMOM - 1, 1)) for step in others]
-    late_all = [to_peer(step, 2, pl.ds(0, NMOM)) for step in others]
+    to_owners = [to_peer(step) for step in others]
 
     def first(vector):
         rows = rows_of(vector)
@@ -364,14 +361,27 @@
     for copy in halos[2]:
         copy.wait_recv()
 
-    def eighth(vector):
-        rows = rows_of(vector)
-        term = hop(4, [gather_ghost(ghost.at[1], row) for row in rows])
-        term_b = hop(4, [gather_ghost(ghost.at[1], 16 + row) for row in rows])
-        for orbital, row in enumerate(rows):
-            change[row], change[16 + row] = 2.0 * term[orbital], 2.0 * term_b[orbital]
-            c_all[2, row] = c_all[2, row] + geo[4, 7] * term[orbital]
-            b_all[2, row] = b_all[2, row] + 2.0 * term_b[orbital]
+    middle_pairs = [(2, m) for m in range(3)] + [(n, 2) for n in range(2)]
+
+    def eighth():
+        sums = [None] * len(middle_pairs)
+        for vector in range(4):
+            rows = rows_of(vector)
+            term = hop(4, [gather_ghost(ghost.at[1], row) for row in rows])
+            term_b = hop(4, [gather_ghost(ghost.at[1], 16 + row) for row in rows])
+            for orbital, row in enumerate(rows):
+                change_a, change_b = 2.0 * term[orbital], 2.0 * term_b[orbital]
+                change[row], change[16 + row] = change_a, change_b
+                c_two = c_all[2, row] + geo[4, 7] * term[orbital]
+                b_two = b_all[2, row] + change_b
+                c_all[2, row], b_all[2, row] = c_two, b_two
+                b_rows = [b_all[0, row], b_all[1, row], b_two]
+                c_rows = [b_rows[0], c_all[1, row], c_two]
+                for at, (n, m) in enumerate(middle_pairs):
+                    part = b_rows[n] * c_rows[m]
+                    sums[at] = part if sums[at] is None else sums[at] + part
+        for (n, m), total in zip(middle_pairs, sums):
+            mom[n, m] = total
 
     def ninth(vector):
         rows = rows_of(vector)
@@ -397,24 +407,16 @@
         for (n, m), total in zip(last_pairs, sums):
             mom[n, m] = total
 
-    loop_flat(eighth)
+    eighth()
     loop_flat(ninth)
-    moments_of(2)
-    for copy, only in zip(early, owns_last):
-        pl.when(jnp.logical_not(only))(copy.start)
     for copy in halos[3]:
         copy.wait_recv()
     tenth()
 
-    for copy, only in zip(late_all, owns_last):
-        pl.when(only)(copy.start)
-    for copy, only in zip(late_one, owns_last):
-        pl.when(jnp.logical_not(only))(copy.start)
-    mine = tile == NMOM - 1
-    for copy in late_all:
-        pl.when(mine)(copy.wait_recv)
-    for copy in late_one + early:
-        pl.when(jnp.logical_not(mine))(copy.wait_recv)
+    for copy in to_owners:
+        copy.start()
+    for copy in to_owners:
+        copy.wait_recv()
     for m in range(NMOM):
         total = mom[tile, m]
         for other in range(ntile - 1):
@@ -423,9 +425,8 @@
     for group in halos:
         for copy in group:
             copy.wait_send()
-    for copies, when in ((late_all, True), (late_one, False), (early, False)):
-        for copy, only in zip(copies, owns_last):
-            pl.when(only if when else jnp.logical_not(only))(copy.wait_send)
+    for copy in to_owners:
+        copy.wait_send()
 
 
 def body(ndom, ntile, vectors, positions, onsite, neighbors):
@@ -454,8 +455,8 @@
             pltpu.SemaphoreType.DMA((4,)),
             pltpu.SemaphoreType.DMA((4, 2)),
             pltpu.SemaphoreType.DMA((4, 2)),
-            pltpu.SemaphoreType.DMA((3, ntile - 1)),
-            pltpu.SemaphoreType.DMA((3, ntile - 1)),
+            pltpu.SemaphoreType.DMA((ntile - 1,)),
+            pltpu.SemaphoreType.DMA((ntile - 1,)),
         ],
         compiler_params=pltpu.CompilerParams(
             collective_id=0, has_side_effects=True, vmem_limit_bytes=16 * 1024 * 1024

time: 26.1 us -> 26 us (level)
  no operation moved by 1% of the time
where the time goes in v6:
time: 26 us; the launch traced here: 25.8 us
  Pallas kernels  25.2 us (97%)
  local copies, waits for them, and re-layouts  0.61 us (2%)
    pallas_call x1, Pallas kernels, body(): pl.pallas_call(functools.partial(kernel, ndom, ntile), out_shape=jax.Shap...  25.2 us
    unnamed x1, local copies, waits for them, and re-layouts  0.61 us

profile of v6, /device:TPU:8, one launch (start us, length us, event | category | flops | bytes accessed | tf_op | source)
XLA Modules:
  0.0 25.8 jit_solution(12167672237777383375)
XLA Ops:
  0.0 25.2 %shard_map.46 = f32[4,8,128]{2,1,0:T(8,128)S(1)} custom-call(f32[4,4,1024]{2,1,0:T(4,128)} %vec_hbm.1, f32[3,1024]{1,0:T(4,128)} %pos_hbm.1, f32[4,1024]{1,0:T(4,128)} %ons_hbm.1, s32[4,1024]{1,0:T(4,128)} %nei_hbm.1), custom_call_target="tpu_custom_call" | custom-call | flops 10000000 | bytes 150000 | tf_op jit(solution)/shard_map/pallas_call | solution.py:437
  25.2 0.6 %copy.7 = f32[1,4,8,128]{3,1,2,0:T(4,128)} copy(f32[1,4,8,128]{3,2,1,0:T(8,128)S(1)} %bitcast.4) | data formatting | bytes 32768
